TPU v7x, 256 devices: a whole 4x4x8 slice. The times are simulated.
256 devices in a mesh: gx: 16 (over y, x), gy: 16 (over z, core).
Axes of the slice: x: 4, y: 4, z: 8, core: 2. Of those that a mesh axis runs over, the one named last changes fastest.
Arguments:
- head_start: float32 [512, 256, 128], P('gx', 'gy'), may hold values from -6 to 6
- recharge: float32 [512, 256, 128], P('gx', 'gy'), may hold values from -12 to 12
- conductivity: float32 [512, 256, 128], P('gx', 'gy'), may hold values from 0.1 to 10
Outputs:
- head: float32 [512, 256, 128], P('gx', 'gy')
All inputs are finite; a program needn't handle non-finite values.
Results may differ from a plain program's by a relative error of at most 0.0003.
Values sent between devices are 32-bit elements; how exact they have to be, the bound alone decides.
A program may use at most 64 MiB of HBM per device.

v0:
```python
import jax
import jax.numpy as jnp
from jax import lax
from jax.sharding import PartitionSpec as P

LEVELS = 6
AGGLOM = 3
SWEEPS = 2
COARSE_SWEEPS = 16


OMEGA = 0.8


def extended(block, sides, width):
    for axis, dim in sides:
        count = lax.axis_size(axis)
        forward = [(i, i + 1) for i in range(count - 1)]
        backward = [(target, source) for source, target in forward]
        low = lax.ppermute(
            lax.slice_in_dim(block, block.shape[dim] - width, None, axis=dim), axis, forward
        )
        high = lax.ppermute(lax.slice_in_dim(block, 0, width, axis=dim), axis, backward)
        block = jnp.concatenate([low, block, high], axis=dim)
    return block


def edge_mean(left, right):
    first = jnp.where(left > 0, left, right)
    second = jnp.where(right > 0, right, left)
    return 2.0 * first * second / (first + second)


def face_terms(padded_k):
    face_x = edge_mean(padded_k[:-1, 1:-1, 1:-1], padded_k[1:, 1:-1, 1:-1])
    face_y = edge_mean(padded_k[1:-1, :-1, 1:-1], padded_k[1:-1, 1:, 1:-1])
    face_z = edge_mean(padded_k[1:-1, 1:-1, :-1], padded_k[1:-1, 1:-1, 1:])
    diagonal = (
        face_x[1:]
        + face_x[:-1]
        + face_y[:, 1:]
        + face_y[:, :-1]
        + face_z[:, :, 1:]
        + face_z[:, :, :-1]
    )
    return (face_x, face_y, face_z, diagonal)


def operate(padded, terms, factor):
    face_x, face_y, face_z, diagonal = terms
    inner = padded[1:-1, 1:-1, 1:-1]
    beside_all = face_x[1:] * padded[2:, 1:-1, 1:-1] + face_x[:-1] * padded[:-2, 1:-1, 1:-1]
    beside_all = (
        beside_all
        + face_y[:, 1:] * padded[1:-1, 2:, 1:-1]
        + face_y[:, :-1] * padded[1:-1, :-2, 1:-1]
    )
    beside_all = (
        beside_all
        + face_z[:, :, 1:] * padded[1:-1, 1:-1, 2:]
        + face_z[:, :, :-1] * padded[1:-1, 1:-1, :-2]
    )
    return factor * (diagonal * inner - beside_all)


def restrict(field):
    a, b, c = field.shape
    return field.reshape(a // 2, 2, b // 2, 2, c // 2, 2).mean(axis=(1, 3, 5))


def prolong(field):
    a, b, c = field.shape
    wide = jnp.broadcast_to(field[:, None, :, None, :, None], (a, 2, b, 2, c, 2))
    return wide.reshape(2 * a, 2 * b, 2 * c)


def edges(field, layout):
    if layout == "grid":
        field = extended(field, (("gx", 0), ("gy", 1)), 1)
    elif layout == "strip":
        field = extended(field, (("gx", 0),), 1)
        field = jnp.pad(field, ((0, 0), (1, 1), (0, 0)))
    else:
        field = jnp.pad(field, ((1, 1), (1, 1), (0, 0)))
    return jnp.pad(field, ((0, 0), (0, 0), (1, 1)))


def smooth(field, source, terms, factor, sweeps, layout):
    first = 0
    if field is None:
        field = OMEGA * source / (factor * terms[3])
        first = 1

    def one_sweep(index, current):
        residue = source - operate(edges(current, layout), terms, factor)
        return current + OMEGA * residue / (factor * terms[3])

    field = lax.fori_loop(first, sweeps, one_sweep, field)
    return field


def layout_of(level_no):
    if level_no <= AGGLOM:
        return "grid"
    if level_no == AGGLOM + 1:
        return "strip"
    return "local"


def descend(level_no, source, conduct):
    if level_no == AGGLOM:
        strips = (
            lax.all_gather(source, "gy", axis=1, tiled=True),
            lax.all_gather(conduct, "gy", axis=1, tiled=True),
        )
        return (strips[0], strips[1])
    if level_no == AGGLOM + 1:
        whole = (
            lax.all_gather(source, "gx", axis=0, tiled=True),
            lax.all_gather(conduct, "gx", axis=0, tiled=True),
        )
        return (whole[0], whole[1])
    return (source, conduct)


def ascend(coarse, fine_shape):
    half_x = fine_shape[0] // 2
    half_y = fine_shape[1] // 2
    if coarse.shape[0] != half_x:
        start_x = lax.axis_index("gx") * half_x
        coarse = lax.dynamic_slice_in_dim(coarse, start_x, half_x, 0)
    if coarse.shape[1] != half_y:
        start_y = lax.axis_index("gy") * half_y
        coarse = lax.dynamic_slice_in_dim(coarse, start_y, half_y, 1)
    return coarse


def cycle(level_no, field, source, conduct):
    factor = 0.25**level_no
    layout = layout_of(level_no)
    terms = face_terms(edges(conduct, layout))
    if level_no == LEVELS - 1:
        return smooth(None, source, terms, factor, COARSE_SWEEPS, layout)
    field = smooth(field, source, terms, factor, SWEEPS, layout)
    residue = source - operate(edges(field, layout), terms, factor)
    coarse_source, coarse_conduct = descend(level_no, restrict(residue), restrict(conduct))
    coarse = cycle(level_no + 1, None, coarse_source, coarse_conduct)
    field = field + prolong(ascend(coarse, field.shape))
    return smooth(field, source, terms, factor, SWEEPS, layout)


def on_device(head_start, recharge, conductivity):
    return cycle(0, head_start, recharge, conductivity)


def solution(mesh):
    return jax.shard_map(
        on_device,
        mesh=mesh,
        in_specs=(P("gx", "gy", None), P("gx", "gy", None), P("gx", "gy", None)),
        out_specs=P("gx", "gy", None),
        check_vma=False,
    )
```

profile of v0, /device:TPU:1, one launch (start us, length us, event | category | flops | bytes accessed | tf_op | source)
XLA Modules:
  0.0 585.3 jit_solution(18017516990932292218)
XLA Ops:
  6.1 18.8 %reshape.96 = f32[16,2,8,2,64,2]{5,4,3,2,1,0:T(8,128)} reshape(f32[32,16,128]{2,1,0:T(8,128)} %param.19) | data formatting | bytes 524288 | tf_op jit(solution)/shard_map/reshape | solution.py:68
  24.9 7.1 %reduce_sum.101 = f32[16,8,64]{2,1,0:T(8,128)S(1)} reduce(f32[16,2,8,2,64,2]{5,4,3,2,1,0:T(8,128)} %reshape.96, f32[]{:T(128)} %constant.275.clone.1), dimensions={1,3,5}, to_apply=%region_3.4 | reduce | flops 57344 | bytes 294916 | tf_op jit(solution)/shard_map/reduce_sum | solution.py:68
  43.1 21.3 %all-gather.5 = f32[16,8,2]{1,2,0:T(2,128)S(1)} all-gather(f32[1,8,2]{1,2,0:T(2,128)S(1)} %multiply_bitcast_fusion.2), channel_id=3, replica_groups=mesh['gx'=16,'gy'=16] {'gy'}, dimensions={0}, use_global_device_ids=true | all-gather | bytes 1088 | tf_op jit(solution)/shard_map/all_gather | solution.py:114
  64.9 23.1 %all-gather.7 = f32[16,8,4]{1,2,0:T(4,128)S(1)} all-gather(f32[1,8,4]{1,2,0:T(4,128)S(1)} %multiply_bitcast_fusion), channel_id=5, replica_groups=mesh['gx'=16,'gy'=16] {'gx'}, dimensions={0}, use_global_device_ids=true | all-gather | bytes 2176 | tf_op jit(solution)/shard_map/all_gather | solution.py:120
  88.6 7.0 %collective-permute-start.56 = (f32[6,1,16]{2,0,1:T(8,128)S(1)}, f32[6,1,16]{2,0,1:T(8,128)S(1)}, u32[]{:S(2)}, u32[]{:S(2)}) collective-permute-start(f32[6,1,16]{2,0,1:T(8,128)S(1)} %get-tuple-element.947), channel_id=1, source_target_pairs={{0,1},{1,2},{2,3},{3,4},{4,5},{5,6},{6,7},{7,8},{8,9},{9,10},{10,1... | collective-permute-start | bytes 1160 | tf_op jit(solution)/shard_map/ppermute | solution.py:20
  131.4 36.8 %while.100 = (s32[]{:T(128)}, f32[32,16,128]{2,1,0:T(8,128)S(1)}, f32[32,16,128]{2,1,0:T(8,128)S(1)}, f32[33,16,128]{2,1,0:T(8,128)S(1)}, f32[32,17,128]{2,1,0:T...) while((s32[]{:T(128)}, f32[32,16,128]{2,1,0:T(8,128)S(1)}, ...), condition=%wide.region_1.2_spmd, body=%wide.region_0.1_spmd.sunk | while | flops 2012738 | bytes 5495829 | solution.py:98
  187.5 18.1 %reshape.95 = f32[16,2,8,2,64,2]{5,4,3,2,1,0:T(8,128)} reshape(f32[32,16,128]{2,1,0:T(8,128)S(1)} %fusion.104) | data formatting | bytes 524288 | tf_op jit(solution)/shard_map/reshape | solution.py:68
  205.5 7.0 %reduce_sum.97 = f32[16,8,64]{2,1,0:T(8,128)S(1)} reduce(f32[16,2,8,2,64,2]{5,4,3,2,1,0:T(8,128)} %reshape.95, f32[]{:T(128)} %constant.275.clone.1), dimensions={1,3,5}, to_apply=%region_2.3 | reduce | flops 57344 | bytes 294916 | tf_op jit(solution)/shard_map/reduce_sum | solution.py:68
  267.1 6.2 %collective-permute-start.51 = (f32[1,4,32]{2,1,0:T(4,128)S(1)}, f32[1,4,32]{2,1,0:T(4,128)S(1)}, u32[]{:S(2)}, u32[]{:S(2)}) collective-permute-start(f32[1,4,32]{2,1,0:T(4,128)S(1)} %get-tuple-element.937), channel_id=1, source_target_pairs={{0,16},{16,32},{32,48},{48,64},{64,80},{80,96},{96,112},{112,128},... | collective-permute-start | bytes 1544 | tf_op jit(solution)/shard_map/ppermute | solution.py:20
  283.6 6.4 %collective-permute-start.59 = (f32[1,2,16]{2,0,1:T(1,128)S(1)}, f32[1,2,16]{2,0,1:T(1,128)S(1)}, u32[]{:S(2)}, u32[]{:S(2)}) collective-permute-start(f32[1,2,16]{2,0,1:T(1,128)S(1)} %get-tuple-element.958), channel_id=1, source_target_pairs={{0,16},{16,32},{32,48},{48,64},{64,80},{80,96},{96,112},{112,128},... | collective-permute-start | bytes 392 | tf_op jit(solution)/shard_map/while/body/eval_jaxpr/ppermute | solution.py:20
  299.9 6.6 %collective-permute-start.63 = (f32[1,2,16]{2,0,1:T(1,128)S(1)}, f32[1,2,16]{2,0,1:T(1,128)S(1)}, u32[]{:S(2)}, u32[]{:S(2)}) collective-permute-start(f32[1,2,16]{2,0,1:T(1,128)S(1)} %get-tuple-element.956), channel_id=1, source_target_pairs={{0,16},{16,32},{32,48},{48,64},{64,80},{80,96},{96,112},{112,128},... | collective-permute-start | bytes 392 | tf_op jit(solution)/shard_map/ppermute | solution.py:20
  315.4 31.7 %all-gather.4 = f32[16,8,2]{1,2,0:T(2,128)S(1)} all-gather(f32[1,8,2]{1,2,0:T(2,128)S(1)} %multiply_bitcast_fusion.3), channel_id=2, replica_groups=mesh['gx'=16,'gy'=16] {'gy'}, dimensions={0}, use_global_device_ids=true | all-gather | bytes 1088 | tf_op jit(solution)/shard_map/all_gather | solution.py:113
  348.7 6.6 %collective-permute-start.69 = (f32[1,16,8]{2,1,0:T(8,128)S(1)}, f32[1,16,8]{2,1,0:T(8,128)S(1)}, u32[]{:S(2)}, u32[]{:S(2)}) collective-permute-start(f32[1,16,8]{2,1,0:T(8,128)S(1)} %get-tuple-element.933), channel_id=1, source_target_pairs={{0,16},{16,32},{32,48},{48,64},{64,80},{80,96},{96,112},{112,128},... | collective-permute-start | bytes 1544 | tf_op jit(solution)/shard_map/while/body/eval_jaxpr/ppermute | solution.py:20
  357.5 6.6 %collective-permute-start.71 = (f32[1,16,8]{2,1,0:T(8,128)S(1)}, f32[1,16,8]{2,1,0:T(8,128)S(1)}, u32[]{:S(2)}, u32[]{:S(2)}) collective-permute-start(f32[1,16,8]{2,1,0:T(8,128)S(1)} %get-tuple-element.931), channel_id=1, source_target_pairs={{0,16},{16,32},{32,48},{48,64},{64,80},{80,96},{96,112},{112,128},... | collective-permute-start | bytes 1544 | tf_op jit(solution)/shard_map/ppermute | solution.py:20
  365.3 28.4 %all-gather.6 = f32[16,8,4]{1,2,0:T(4,128)S(1)} all-gather(f32[1,8,4]{1,2,0:T(4,128)S(1)} %multiply_bitcast_fusion.1), channel_id=4, replica_groups=mesh['gx'=16,'gy'=16] {'gx'}, dimensions={0}, use_global_device_ids=true | all-gather | bytes 2176 | tf_op jit(solution)/shard_map/all_gather | solution.py:119
  398.1 12.7 %while.102 = (s32[]{:T(128)}, f32[2,16,8]{1,2,0:T(8,128)S(1)}, f32[2,16,8]{1,2,0:T(8,128)S(1)}, f32[3,16,8]{1,2,0:T(8,128)S(1)}, f32[2,17,8]{1,2,0:T(8,128)S(1)}...) while((s32[]{:T(128)}, f32[2,16,8]{1,2,0:T(8,128)S(1)}, f32[2,16,8]{1,2,0:T(8,128)S(1)}, ...), condition=%wide.region_19.20_spmd, body=%wide.region_18.19_spmd.sunk | while | flops 9986 | bytes 128421 | solution.py:98
  411.1 45.4 %while.103 = (s32[]{:T(128)}, f32[4,2,16]{2,1,0:T(2,128)S(1)}, f32[4,2,16]{2,1,0:T(2,128)S(1)}, f32[5,2,16]{2,1,0:T(2,128)S(1)}, f32[4,3,16]{2,1,0:T(4,128)S(1)}...) while((s32[]{:T(128)}, f32[4,2,16]{2,1,0:T(2,128)S(1)}, f32[4,2,16]{2,1,0:T(2,128)S(1)}, ...), condition=%wide.region_21.22_spmd, body=%wide.region_20.21_spmd.sunk | while | flops 6402 | bytes 30005 | solution.py:98
  419.0 13.9 %collective-permute-start.8 = (f32[6,1,16]{2,1,0:T(1,128)S(1)}, f32[6,1,16]{2,1,0:T(1,128)S(1)}, u32[]{:S(2)}, u32[]{:S(2)}) collective-permute-start(f32[6,1,16]{2,1,0:T(1,128)S(1)} %get-tuple-element.1272), channel_id=1, source_target_pairs={{1,0},{2,1},{3,2},{4,3},{5,4},{6,5},{7,6},{8,7},{9,8},{10,9},{11,1... | collective-permute-start | bytes 1160 | tf_op jit(solution)/shard_map/while/body/eval_jaxpr/ppermute | solution.py:23
  456.7 35.3 %while.104 = (s32[]{:T(128)}, f32[8,4,32]{2,1,0:T(4,128)S(1)}, f32[8,4,32]{2,1,0:T(4,128)S(1)}, f32[9,4,32]{2,1,0:T(4,128)S(1)}, f32[8,5,32]{2,1,0:T(8,128)S(1)}...) while((s32[]{:T(128)}, f32[8,4,32]{2,1,0:T(4,128)S(1)}, f32[8,4,32]{2,1,0:T(4,128)S(1)}, ...), condition=%wide.region_23.24_spmd, body=%wide.region_22.23_spmd.sunk | while | flops 39874 | bytes 143061 | solution.py:98
  456.8 5.7 collective-permute-start.10
  496.9 33.6 %while.105 = (s32[]{:T(128)}, f32[16,8,64]{2,1,0:T(8,128)S(1)}, f32[16,8,64]{2,1,0:T(8,128)S(1)}, f32[17,8,64]{2,1,0:T(8,128)S(1)}, f32[16,9,64]{2,1,0:T(8,128)S...) while((s32[]{:T(128)}, f32[16,8,64]{2,1,0:T(8,128)S(1)}, ...), condition=%wide.region_25.26_spmd, body=%wide.region_24.25_spmd.sunk | while | flops 283458 | bytes 828053 | solution.py:98
  530.5 6.5 %broadcast_in_dim.52 = f32[16,2,8,2,64,2]{5,4,3,2,1,0:T(8,128)} broadcast(f32[16,8,64]{2,1,0:T(8,128)S(1)} %get-tuple-element.717), dimensions={0,2,4} | broadcast | bytes 294912 | tf_op jit(solution)/shard_map/broadcast_in_dim | solution.py:73
  537.0 12.6 %reshape.101 = f32[32,16,128]{2,1,0:T(8,128)S(1)} reshape(f32[16,2,8,2,64,2]{5,4,3,2,1,0:T(8,128)} %broadcast_in_dim.52) | data formatting | bytes 524288 | tf_op jit(solution)/shard_map/reshape | solution.py:74
  549.7 35.0 %while.106 = (s32[]{:T(128)}, f32[32,16,128]{2,1,0:T(8,128)S(1)}, f32[32,16,128]{2,1,0:T(8,128)S(1)}, f32[33,16,128]{2,1,0:T(8,128)S(1)}, f32[32,17,128]{2,1,0:T...) while((s32[]{:T(128)}, f32[32,16,128]{2,1,0:T(8,128)S(1)}, ...), condition=%wide.region_27.28_spmd, body=%wide.region_26.27_spmd.sunk | while | flops 2012738 | bytes 5495829 | solution.py:98
  (465 shorter events, 352.3 us)
Async XLA Ops:
  0.7 120.5 %collective-permute-start.22 = (f32[1,16,128]{2,1,0:T(8,128)S(1)}, f32[1,16,128]{2,1,0:T(8,128)S(1)}, u32[]{:S(2)}, u32[]{:S(2)}) collective-permute-start(f32[1,16,128]{2,1,0:T(8,128)S(1)} %get-tuple-element.910), channel_id=1, source_target_pairs={{0,16},{16,32},{32,48},{48,64},{64,80},{80,96},{96,112},{112,128},... | collective-permute-start | bytes 24584 | tf_op jit(solution)/shard_map/ppermute | solution.py:20
  4.7 116.6 %collective-permute-start.23 = (f32[1,16,128]{2,1,0:T(8,128)S(1)}, f32[1,16,128]{2,1,0:T(8,128)S(1)}, u32[]{:S(2)}, u32[]{:S(2)}) collective-permute-start(f32[1,16,128]{2,1,0:T(8,128)S(1)} %get-tuple-element.909), channel_id=1, source_target_pairs={{16,0},{32,16},{48,32},{64,48},{80,64},{96,80},{112,96},{128,112},... | collective-permute-start | bytes 24584 | tf_op jit(solution)/shard_map/ppermute | solution.py:23
  37.6 50.9 %collective-permute-start.54 = (f32[1,2,16]{2,0,1:T(1,128)S(1)}, f32[1,2,16]{2,0,1:T(1,128)S(1)}, u32[]{:S(2)}, u32[]{:S(2)}) collective-permute-start(f32[1,2,16]{2,0,1:T(1,128)S(1)} %get-tuple-element.960), channel_id=1, source_target_pairs={{0,16},{16,32},{32,48},{48,64},{64,80},{80,96},{96,112},{112,128},... | collective-permute-start | bytes 392 | tf_op jit(solution)/shard_map/ppermute | solution.py:20
  41.6 46.9 %collective-permute-start.55 = (f32[1,2,16]{2,0,1:T(1,128)S(1)}, f32[1,2,16]{2,0,1:T(1,128)S(1)}, u32[]{:S(2)}, u32[]{:S(2)}) collective-permute-start(f32[1,2,16]{2,0,1:T(1,128)S(1)} %get-tuple-element.961), channel_id=1, source_target_pairs={{16,0},{32,16},{48,32},{64,48},{80,64},{96,80},{112,96},{128,112},... | collective-permute-start | bytes 392 | tf_op jit(solution)/shard_map/ppermute | solution.py:23
  88.6 10.3 %collective-permute-start.56 = (f32[6,1,16]{2,0,1:T(8,128)S(1)}, f32[6,1,16]{2,0,1:T(8,128)S(1)}, u32[]{:S(2)}, u32[]{:S(2)}) collective-permute-start(f32[6,1,16]{2,0,1:T(8,128)S(1)} %get-tuple-element.947), channel_id=1, source_target_pairs={{0,1},{1,2},{2,3},{3,4},{4,5},{5,6},{6,7},{7,8},{8,9},{9,10},{10,1... | collective-permute-start | bytes 1160 | tf_op jit(solution)/shard_map/ppermute | solution.py:20
  108.7 11.0 %collective-permute-start.32 = (f32[18,1,64]{2,1,0:T(1,128)S(1)}, f32[18,1,64]{2,1,0:T(1,128)S(1)}, u32[]{:S(2)}, u32[]{:S(2)}) collective-permute-start(f32[18,1,64]{2,1,0:T(1,128)S(1)} %get-tuple-element.915), channel_id=1, source_target_pairs={{0,1},{1,2},{2,3},{3,4},{4,5},{5,6},{6,7},{7,8},{8,9},{9,10},{10,1... | collective-permute-start | bytes 13832 | tf_op jit(solution)/shard_map/ppermute | solution.py:20
  116.2 140.9 %collective-permute-start.66 = (f32[1,16,8]{2,1,0:T(8,128)S(1)}, f32[1,16,8]{2,1,0:T(8,128)S(1)}, u32[]{:S(2)}, u32[]{:S(2)}) collective-permute-start(f32[1,16,8]{2,1,0:T(8,128)S(1)} %reshape.107), channel_id=1, source_target_pairs={{0,16},{16,32},{32,48},{48,64},{64,80},{80,96},{96,112},{112,128},... | collective-permute-start | bytes 1544 | tf_op jit(solution)/shard_map/ppermute | solution.py:20
  119.7 153.6 %collective-permute-start.67 = (f32[1,16,8]{2,1,0:T(8,128)S(1)}, f32[1,16,8]{2,1,0:T(8,128)S(1)}, u32[]{:S(2)}, u32[]{:S(2)}) collective-permute-start(f32[1,16,8]{2,1,0:T(8,128)S(1)} %reshape.108), channel_id=1, source_target_pairs={{16,0},{32,16},{48,32},{64,48},{80,64},{96,80},{112,96},{128,112},... | collective-permute-start | bytes 1544 | tf_op jit(solution)/shard_map/ppermute | solution.py:23
  159.2 7.3 %collective-permute-start.2 = (f32[34,1,128]{2,1,0:T(1,128)S(1)}, f32[34,1,128]{2,1,0:T(1,128)S(1)}, u32[]{:S(2)}, u32[]{:S(2)}) collective-permute-start(f32[34,1,128]{2,1,0:T(1,128)S(1)} %get-tuple-element.1245), channel_id=1, source_target_pairs={{1,0},{2,1},{3,2},{4,3},{5,4},{6,5},{7,6},{8,7},{9,8},{10,9},{11,1... | collective-permute-start | bytes 52232 | tf_op jit(solution)/shard_map/while/body/eval_jaxpr/ppermute | solution.py:23
  178.5 7.6 %collective-permute-start.28 = (f32[34,1,128]{2,1,0:T(1,128)S(1)}, f32[34,1,128]{2,1,0:T(1,128)S(1)}, u32[]{:S(2)}, u32[]{:S(2)}) collective-permute-start(f32[34,1,128]{2,1,0:T(1,128)S(1)} %get-tuple-element.901), channel_id=1, source_target_pairs={{1,0},{2,1},{3,2},{4,3},{5,4},{6,5},{7,6},{8,7},{9,8},{10,9},{11,1... | collective-permute-start | bytes 52232 | tf_op jit(solution)/shard_map/ppermute | solution.py:23
  212.7 10.2 %collective-permute-start.34 = (f32[1,8,64]{2,1,0:T(8,128)S(1)}, f32[1,8,64]{2,1,0:T(8,128)S(1)}, u32[]{:S(2)}, u32[]{:S(2)}) collective-permute-start(f32[1,8,64]{2,1,0:T(8,128)S(1)} %get-tuple-element.921), channel_id=1, source_target_pairs={{16,0},{32,16},{48,32},{64,48},{80,64},{96,80},{112,96},{128,112},... | collective-permute-start | bytes 6152 | tf_op jit(solution)/shard_map/while/body/eval_jaxpr/ppermute | solution.py:23
  214.0 10.9 %collective-permute-start.35 = (f32[1,8,64]{2,1,0:T(8,128)S(1)}, f32[1,8,64]{2,1,0:T(8,128)S(1)}, u32[]{:S(2)}, u32[]{:S(2)}) collective-permute-start(f32[1,8,64]{2,1,0:T(8,128)S(1)} %get-tuple-element.920), channel_id=1, source_target_pairs={{0,16},{16,32},{32,48},{48,64},{64,80},{80,96},{96,112},{112,128},... | collective-permute-start | bytes 6152 | tf_op jit(solution)/shard_map/while/body/eval_jaxpr/ppermute | solution.py:20
  218.4 8.4 %collective-permute-start.44 = (f32[10,1,32]{2,1,0:T(1,128)S(1)}, f32[10,1,32]{2,1,0:T(1,128)S(1)}, u32[]{:S(2)}, u32[]{:S(2)}) collective-permute-start(f32[10,1,32]{2,1,0:T(1,128)S(1)} %get-tuple-element.928), channel_id=1, source_target_pairs={{0,1},{1,2},{2,3},{3,4},{4,5},{5,6},{6,7},{7,8},{8,9},{9,10},{10,1... | collective-permute-start | bytes 3848 | tf_op jit(solution)/shard_map/ppermute | solution.py:20
  222.9 7.6 %collective-permute-start.45 = (f32[10,1,32]{2,1,0:T(1,128)S(1)}, f32[10,1,32]{2,1,0:T(1,128)S(1)}, u32[]{:S(2)}, u32[]{:S(2)}) collective-permute-start(f32[10,1,32]{2,1,0:T(1,128)S(1)} %get-tuple-element.929), channel_id=1, source_target_pairs={{1,0},{2,1},{3,2},{4,3},{5,4},{6,5},{7,6},{8,7},{9,8},{10,9},{11,1... | collective-permute-start | bytes 3848 | tf_op jit(solution)/shard_map/ppermute | solution.py:23
  265.8 7.6 %collective-permute-start.50 = (f32[1,4,32]{2,1,0:T(4,128)S(1)}, f32[1,4,32]{2,1,0:T(4,128)S(1)}, u32[]{:S(2)}, u32[]{:S(2)}) collective-permute-start(f32[1,4,32]{2,1,0:T(4,128)S(1)} %get-tuple-element.938), channel_id=1, source_target_pairs={{16,0},{32,16},{48,32},{64,48},{80,64},{96,80},{112,96},{128,112},... | collective-permute-start | bytes 1544 | tf_op jit(solution)/shard_map/ppermute | solution.py:23
  282.3 7.7 %collective-permute-start.58 = (f32[1,2,16]{2,0,1:T(1,128)S(1)}, f32[1,2,16]{2,0,1:T(1,128)S(1)}, u32[]{:S(2)}, u32[]{:S(2)}) collective-permute-start(f32[1,2,16]{2,0,1:T(1,128)S(1)} %get-tuple-element.959), channel_id=1, source_target_pairs={{16,0},{32,16},{48,32},{64,48},{80,64},{96,80},{112,96},{128,112},... | collective-permute-start | bytes 392 | tf_op jit(solution)/shard_map/while/body/eval_jaxpr/ppermute | solution.py:23
  298.6 8.0 %collective-permute-start.62 = (f32[1,2,16]{2,0,1:T(1,128)S(1)}, f32[1,2,16]{2,0,1:T(1,128)S(1)}, u32[]{:S(2)}, u32[]{:S(2)}) collective-permute-start(f32[1,2,16]{2,0,1:T(1,128)S(1)} %get-tuple-element.957), channel_id=1, source_target_pairs={{16,0},{32,16},{48,32},{64,48},{80,64},{96,80},{112,96},{128,112},... | collective-permute-start | bytes 392 | tf_op jit(solution)/shard_map/ppermute | solution.py:23
  299.9 7.4 %collective-permute-start.63 = (f32[1,2,16]{2,0,1:T(1,128)S(1)}, f32[1,2,16]{2,0,1:T(1,128)S(1)}, u32[]{:S(2)}, u32[]{:S(2)}) collective-permute-start(f32[1,2,16]{2,0,1:T(1,128)S(1)} %get-tuple-element.956), channel_id=1, source_target_pairs={{0,16},{16,32},{32,48},{48,64},{64,80},{80,96},{96,112},{112,128},... | collective-permute-start | bytes 392 | tf_op jit(solution)/shard_map/ppermute | solution.py:20
  347.4 8.3 %collective-permute-start.68 = (f32[1,16,8]{2,1,0:T(8,128)S(1)}, f32[1,16,8]{2,1,0:T(8,128)S(1)}, u32[]{:S(2)}, u32[]{:S(2)}) collective-permute-start(f32[1,16,8]{2,1,0:T(8,128)S(1)} %get-tuple-element.934), channel_id=1, source_target_pairs={{16,0},{32,16},{48,32},{64,48},{80,64},{96,80},{112,96},{128,112},... | collective-permute-start | bytes 1544 | tf_op jit(solution)/shard_map/while/body/eval_jaxpr/ppermute | solution.py:23
  348.7 7.4 %collective-permute-start.69 = (f32[1,16,8]{2,1,0:T(8,128)S(1)}, f32[1,16,8]{2,1,0:T(8,128)S(1)}, u32[]{:S(2)}, u32[]{:S(2)}) collective-permute-start(f32[1,16,8]{2,1,0:T(8,128)S(1)} %get-tuple-element.933), channel_id=1, source_target_pairs={{0,16},{16,32},{32,48},{48,64},{64,80},{80,96},{96,112},{112,128},... | collective-permute-start | bytes 1544 | tf_op jit(solution)/shard_map/while/body/eval_jaxpr/ppermute | solution.py:20
  356.2 8.3 %collective-permute-start.70 = (f32[1,16,8]{2,1,0:T(8,128)S(1)}, f32[1,16,8]{2,1,0:T(8,128)S(1)}, u32[]{:S(2)}, u32[]{:S(2)}) collective-permute-start(f32[1,16,8]{2,1,0:T(8,128)S(1)} %get-tuple-element.932), channel_id=1, source_target_pairs={{16,0},{32,16},{48,32},{64,48},{80,64},{96,80},{112,96},{128,112},... | collective-permute-start | bytes 1544 | tf_op jit(solution)/shard_map/ppermute | solution.py:23
  357.5 7.4 %collective-permute-start.71 = (f32[1,16,8]{2,1,0:T(8,128)S(1)}, f32[1,16,8]{2,1,0:T(8,128)S(1)}, u32[]{:S(2)}, u32[]{:S(2)}) collective-permute-start(f32[1,16,8]{2,1,0:T(8,128)S(1)} %get-tuple-element.931), channel_id=1, source_target_pairs={{0,16},{16,32},{32,48},{48,64},{64,80},{80,96},{96,112},{112,128},... | collective-permute-start | bytes 1544 | tf_op jit(solution)/shard_map/ppermute | solution.py:20
  419.0 17.1 %collective-permute-start.8 = (f32[6,1,16]{2,1,0:T(1,128)S(1)}, f32[6,1,16]{2,1,0:T(1,128)S(1)}, u32[]{:S(2)}, u32[]{:S(2)}) collective-permute-start(f32[6,1,16]{2,1,0:T(1,128)S(1)} %get-tuple-element.1272), channel_id=1, source_target_pairs={{1,0},{2,1},{3,2},{4,3},{5,4},{6,5},{7,6},{8,7},{9,8},{10,9},{11,1... | collective-permute-start | bytes 1160 | tf_op jit(solution)/shard_map/while/body/eval_jaxpr/ppermute | solution.py:23
  575.7 7.3 %collective-permute-start.20 = (f32[34,1,128]{2,1,0:T(1,128)S(1)}, f32[34,1,128]{2,1,0:T(1,128)S(1)}, u32[]{:S(2)}, u32[]{:S(2)}) collective-permute-start(f32[34,1,128]{2,1,0:T(1,128)S(1)} %get-tuple-element.1305), channel_id=1, source_target_pairs={{1,0},{2,1},{3,2},{4,3},{5,4},{6,5},{7,6},{8,7},{9,8},{10,9},{11,1... | collective-permute-start | bytes 52232 | tf_op jit(solution)/shard_map/while/body/eval_jaxpr/ppermute | solution.py:23
  (74 other events, 735.6 us)
where the time goes:
time: 597 us; the launch traced here: 585 us
  starting transfers between devices  308 us (52%)
  blocking collectives  105 us (18%)
  local copies, waits for them, and re-layouts  74.5 us (12%)
  waiting for transfers between devices  65.5 us (11%)
  other arithmetic  30.5 us (5%)
    ppermute x47, starting transfers between devices, extended(): lax.ppermute(lax.slice_in_dim(block, block.shape[dim] - width, None, axis...  221 us
    ppermute x47, starting transfers between devices, extended(): lax.ppermute(lax.slice_in_dim(block, 0, width, axis=dim), axis, backward)  86.4 us
    ppermute x47, waiting for transfers between devices, extended(): lax.ppermute(lax.slice_in_dim(block, 0, width, axis=dim), axis, backward)  47.2 us
    reshape x4, local copies, waits for them, and re-layouts, restrict(): return field.reshape(a // 2, 2, b // 2, 2, c // 2, 2).mean(axis=(1, 3, 5))  40.5 us
    all_gather x1, blocking collectives, descend(): lax.all_gather(source, 'gy', axis=1, tiled=True)  31.7 us
    all_gather x1, blocking collectives, descend(): lax.all_gather(source, 'gx', axis=0, tiled=True)  28.4 us
    all_gather x1, blocking collectives, descend(): lax.all_gather(conduct, 'gx', axis=0, tiled=True)  23.1 us
    all_gather x1, blocking collectives, descend(): lax.all_gather(conduct, 'gy', axis=1, tiled=True)  21.3 us
  transfers between devices with their start and end apart: 94, of which 40 were waited for; matrix products, arithmetic and copies ran while one was open for 12% of the time, Pallas kernels for 0%

commit v1 on v0

v1 whole, which is shorter than its diff:
```python
from typing import NamedTuple

import jax
import jax.numpy as jnp
from jax import lax
from jax.experimental import pallas as pl
from jax.experimental.pallas import tpu as pltpu
from jax.sharding import PartitionSpec as P

F32 = jnp.float32
LANES = 128
PAD = 8
OMEGA = 0.8
KEEP = 1.0 - OMEGA
COARSE_SWEEPS = 16
BLOCK_X = 32
BLOCK_Y = 16
TALLY_ROWS = 512

class Level(NamedTuple):
    bx: int
    by: int
    hx: int
    rows: int
    first: int
    span: int
    reach: int
    hk: int
    hg: int
    cyrows: int


SPLIT = (
    Level(32, 16, 3, 24, 4, 1, 1, 4, 3, 24),
    Level(16, 8, 4, 16, 4, 2, 1, 5, 4, 24),
    Level(8, 4, 5, 16, 6, 4, 2, 6, 5, 16),
)


def reciprocal(x):
    guess = pltpu.reciprocal(x, approx=True)
    return guess * (2.0 - x * guess)


def face(a, b):
    return (2.0 * a * b) * reciprocal(a + b)


def iota(shape, dim):
    return lax.broadcasted_iota(jnp.int32, shape, dim)


def flag(condition):
    return jnp.where(condition, 1.0, 0.0).astype(F32)


def up(value, shift):
    return pltpu.roll(value, LANES - shift, value.ndim - 1)


def down(value, shift):
    return pltpu.roll(value, shift, value.ndim - 1)


def swap(value, bit):
    if 2 * bit == LANES:
        return down(value, bit)
    lane = iota(value.shape, value.ndim - 1)
    return jnp.where((lane & bit) == 0, up(value, bit), down(value, bit))


def lane_gather(value, index):
    return jnp.take_along_axis(value, index, axis=1)


def segment(step, block, halo):
    low = max(0, step * block - halo)
    high = min(block, (step + 1) * block + halo)
    return low, high - low, low - step * block


def partners(level, halo):
    for dx in (-1, 0, 1):
        for dy in range(-level.reach, level.reach + 1):
            if (dx, dy) != (0, 0):
                yield dx, dy, segment(dx, level.bx, halo), segment(dy, level.by, halo)


def exchange_rows(level, halo):
    return sum(xs[1] * ys[1] for _, _, xs, ys in partners(level, halo))


class Split:
    def __init__(self, level, nx, ny, gx, gy, refs):
        self.at = level
        self.nx, self.ny, self.gx, self.gy = nx, ny, gx, gy
        (self.k, self.va, self.vb, self.g, self.cx, self.cy, self.czl, self.czh, self.w, self.d) = refs

    @staticmethod
    def scratch(level):
        x, rows = level.bx + 2 * level.hx, level.rows
        padded = pltpu.VMEM((x + 2, rows + 2 * PAD, LANES), F32)
        plain = pltpu.VMEM((x, rows, LANES), F32)
        return [
            padded,
            padded,
            padded,
            plain,
            pltpu.VMEM((x + 1, rows, LANES), F32),
            pltpu.VMEM((x, rows + PAD, LANES), F32),
            plain,
            plain,
            plain,
            plain,
        ]

    def x_cut(self, i):
        x = self.gx * self.at.bx + i - self.at.hx
        return flag((x == 0) | (x == self.nx))

    def faces(self):
        lv = self.at
        count, rows, span = lv.bx + 2 * lv.hx, lv.rows, lv.span
        y = self.gy * lv.by + iota((1, lv.cyrows, LANES), 1) - lv.first
        y_open = flag((y != 0) & (y != self.ny))
        y = y[:, :rows]
        lane = iota((1, rows, LANES), 2)
        z_open = flag(lane >= span)
        cuts = flag((y == 0) | (y == self.ny)) + flag((y == -1) | (y == self.ny - 1))
        cuts = cuts + flag(lane < span) + flag(lane >= LANES - span)
        inner = pl.ds(PAD, rows)

        def step(i, carry):
            here, low_x = carry
            beyond = self.k[pl.ds(i + 2, 1), inner, :]
            cut_low, cut_high = self.x_cut(i), self.x_cut(i + 1)
            high_x = face(here, beyond) * (1.0 - cut_high)
            self.cx[pl.ds(i + 1, 1)] = high_x
            low_y = face(
                self.k[pl.ds(i + 1, 1), pl.ds(PAD - 1, lv.cyrows), :],
                self.k[pl.ds(i + 1, 1), pl.ds(PAD, lv.cyrows), :],
            )
            low_y = low_y * y_open
            self.cy[pl.ds(i, 1), pl.ds(0, lv.cyrows), :] = low_y
            low_z = face(down(here, span), here) * z_open
            high_z = up(low_z, span)
            self.czl[pl.ds(i, 1)] = low_z
            self.czh[pl.ds(i, 1)] = high_z
            high_y = self.cy[pl.ds(i, 1), pl.ds(1, rows), :]
            total = low_x + high_x + low_y[:, :rows] + high_y + low_z + high_z
            total = total + here * (cuts + (cut_low + cut_high))
            self.d[pl.ds(i, 1)] = total
            self.w[pl.ds(i, 1)] = OMEGA * reciprocal(total)
            return beyond, high_x

        start = self.k[pl.ds(1, 1), inner, :]
        edge = face(self.k[pl.ds(0, 1), inner, :], start) * (1.0 - self.x_cut(0))
        self.cx[pl.ds(0, 1)] = edge
        lax.fori_loop(0, count, step, (start, edge), unroll=2)

    def stencil(self, v, low, high, row, rows, use):
        span = self.at.span
        inner = pl.ds(PAD + row, rows)
        own = pl.ds(row, rows)

        def step(i, carry):
            before, here, low_x = carry
            after = v[pl.ds(i + 2, 1), inner, :]
            high_x = self.cx[pl.ds(i + 1, 1), own, :]
            total = low_x * before + high_x * after
            total = total + (
                self.cy[pl.ds(i, 1), own, :] * v[pl.ds(i + 1, 1), pl.ds(PAD + row - 1, rows), :]
                + self.cy[pl.ds(i, 1), pl.ds(row + 1, rows), :]
                * v[pl.ds(i + 1, 1), pl.ds(PAD + row + 1, rows), :]
            )
            total = total + (
                self.czl[pl.ds(i, 1), own, :] * down(here, span)
                + self.czh[pl.ds(i, 1), own, :] * up(here, span)
            )
            use(i, here, total)
            return here, after, high_x

        start = (
            v[pl.ds(low, 1), inner, :],
            v[pl.ds(low + 1, 1), inner, :],
            self.cx[pl.ds(low, 1), own, :],
        )
        lax.fori_loop(low, high, step, start, unroll=2)

    def first_sweep(self, dst):
        count, rows = self.at.bx + 2 * self.at.hx, self.at.rows

        def step(i, carry):
            dst[pl.ds(i + 1, 1), pl.ds(PAD, rows), :] = self.w[pl.ds(i, 1)] * self.g[pl.ds(i, 1)]
            return carry

        lax.fori_loop(0, count, step, 0, unroll=2)

    def sweep(self, src, dst, halo):
        lv = self.at

        def use(i, here, total):
            dst[pl.ds(i + 1, 1), pl.ds(PAD, lv.rows), :] = KEEP * here + self.w[pl.ds(i, 1)] * (
                self.g[pl.ds(i, 1)] + total
            )

        self.stencil(src, lv.hx - halo, lv.hx + lv.bx + halo, 0, lv.rows, use)

    def last_sweep(self, src, out):
        lv = self.at
        own = pl.ds(lv.first, lv.by)

        def use(i, here, total):
            out[pl.ds(i - lv.hx, 1)] = KEEP * here + self.w[pl.ds(i, 1), own, :] * (
                self.g[pl.ds(i, 1), own, :] + total
            )

        self.stencil(src, lv.hx, lv.hx + lv.bx, lv.first, lv.by, use)

    def residual(self, v, out):
        lv = self.at
        own = pl.ds(lv.first, lv.by)

        def use(i, here, total):
            out[pl.ds(i - lv.hx, 1)] = (
                self.g[pl.ds(i, 1), own, :] + total - self.d[pl.ds(i, 1), own, :] * here
            )

        self.stencil(v, lv.hx, lv.hx + lv.bx, lv.first, lv.by, use)

    def correct(self, v, coarse, xlow, xcount, xshift, rowshift, wide):
        lv = self.at
        half = lv.rows // 2

        def step(j, carry):
            rows = coarse(j, rowshift, half)
            wide[pl.ds(j, 1), pl.ds(0, half, stride=2), :] = rows
            wide[pl.ds(j, 1), pl.ds(1, half, stride=2), :] = rows
            copies = wide[pl.ds(j, 1)]
            for child in range(2):
                place = (pl.ds(2 * (xlow + j) + xshift + child, 1), pl.ds(PAD, lv.rows))
                v[place] = v[place] + copies
            return carry

        lax.fori_loop(0, xcount, step, 0, unroll=2)


def restrict(read, count, rows, span, scale, write):
    def step(j, carry):
        total = (read(2 * j, 0) + read(2 * j, 1)) + (read(2 * j + 1, 0) + read(2 * j + 1, 1))
        write(j, scale * (total + swap(total, span)))
        return carry

    lax.fori_loop(0, count, step, 0, unroll=2)


class Whole:
    def __init__(self, number, nx, ny, refs):
        self.number, self.nx, self.ny = number, nx, ny
        self.k, self.va, self.vb, self.g, self.c, self.w, self.d = refs

    @staticmethod
    def scratch(nx, ny):
        padded = pltpu.VMEM((nx + 2, ny + 2 * PAD, LANES), F32)
        plain = pltpu.VMEM((nx, ny, LANES), F32)
        return [padded, padded, padded, plain, pltpu.VMEM((6, nx, ny, LANES), F32), plain, plain]

    def clear_edges(self):
        for ref in (self.k, self.va, self.vb):
            for x in (0, self.nx + 1):
                ref[x] = jnp.zeros((self.ny + 2 * PAD, LANES), F32)
            for row in (0, PAD + self.ny):
                ref[:, pl.ds(row, PAD), :] = jnp.zeros((self.nx + 2, PAD, LANES), F32)

    def neighbours(self, v, i):
        inner = pl.ds(PAD, self.ny)
        here = v[pl.ds(i + 1, 1), inner, :]
        before = v[pl.ds(i, 1), inner, :]
        after = v[pl.ds(i + 2, 1), inner, :]
        under = v[pl.ds(i + 1, 1), pl.ds(PAD - 1, self.ny), :]
        over = v[pl.ds(i + 1, 1), pl.ds(PAD + 1, self.ny), :]
        lane = iota(here.shape, 2)
        if self.number == 3:
            before = down(jnp.where(lane >= 96, before, here), 32)
            after = up(jnp.where(lane < 32, after, here), 32)
            odd = (lane & 16) != 0
            under = swap(jnp.where(odd, under, here), 16)
            over = swap(jnp.where(odd, here, over), 16)
            span = 1
        else:
            before = down(jnp.where(lane >= 64, before, here), 64)
            after = up(jnp.where(lane < 64, after, here), 64)
            span = 2
        return (before, after, under, over, down(here, span), up(here, span)), here

    def faces(self):
        shape = (1, self.ny, LANES)
        lane, row = iota(shape, 2), iota(shape, 1)
        z = lane & 15
        if self.number == 3:
            first_x, last_x, first_y, last_y = lane < 32, lane >= 96, (lane & 16) == 0, (lane & 16) != 0
            first_z, last_z = z == 0, z == 15
            first_y, last_y = (row == 0) & first_y, (row == self.ny - 1) & last_y
        else:
            first_x, last_x, first_y, last_y = lane < 64, lane >= 64, row == 0, row == self.ny - 1
            first_z, last_z = z < 2, z >= 14
        cuts_x = (flag(first_x), flag(last_x))
        cuts_yz = tuple(flag(c) for c in (first_y, last_y, first_z, last_z))

        def step(i, carry):
            sides, here = self.neighbours(self.k, i)
            cuts = (cuts_x[0] * flag(i == 0), cuts_x[1] * flag(i == self.nx - 1)) + cuts_yz
            total = jnp.zeros(shape, F32)
            for n in range(6):
                value = face(here, sides[n]) * (1.0 - cuts[n])
                self.c[n, pl.ds(i, 1)] = value
                total = total + (value + here * cuts[n])
            self.d[pl.ds(i, 1)] = total
            self.w[pl.ds(i, 1)] = OMEGA * reciprocal(total)
            return carry

        lax.fori_loop(0, self.nx, step, 0, unroll=2)

    def beside(self, v, i):
        sides, here = self.neighbours(v, i)
        parts = [self.c[n, pl.ds(i, 1)] * sides[n] for n in range(6)]
        return here, (parts[0] + parts[1]) + (parts[2] + parts[3]) + (parts[4] + parts[5])

    def first_sweep(self, dst):
        dst[pl.ds(1, self.nx), pl.ds(PAD, self.ny), :] = self.w[...] * self.g[...]

    def sweep(self, src, dst):
        def step(i, carry):
            here, total = self.beside(src, i)
            dst[pl.ds(i + 1, 1), pl.ds(PAD, self.ny), :] = KEEP * here + self.w[pl.ds(i, 1)] * (
                self.g[pl.ds(i, 1)] + total
            )
            return carry

        lax.fori_loop(0, self.nx, step, 0, unroll=4)

    def residual(self, v, use):
        def step(i, carry):
            here, total = self.beside(v, i)
            use(i, self.g[pl.ds(i, 1)] + total - self.d[pl.ds(i, 1)] * here)
            return carry

        lax.fori_loop(0, self.nx, step, 0, unroll=4)

    def correct(self, v, rows_of):
        inner = pl.ds(PAD, self.ny)

        def step(i, carry):
            v[pl.ds(i + 1, 1), inner, :] = v[pl.ds(i + 1, 1), inner, :] + rows_of(i)
            return carry

        lax.fori_loop(0, self.nx, step, 0, unroll=4)


def octet_3(value):
    value = value + swap(value, 1)
    value = value + swap(value, 16)
    return value + swap(value, 32)


def pack_5(ref, fill, scale, nx, ny):
    half = ny // 2
    shape = (half, LANES)
    lane = iota(shape, 1)
    index = (lane & 3) * 4
    packed = jnp.full(shape, fill, F32)
    for i in range(nx):
        rows = ref[i, pl.ds(0, half, stride=2), :] + ref[i, pl.ds(1, half, stride=2), :]
        rows = rows + swap(rows, 2)
        rows = scale * (rows + swap(rows, 64))
        packed = jnp.where((lane >> 2) == i, lane_gather(rows, index), packed)
    return packed


def solve_5(k, g, nx):
    shape = k.shape
    lane, row = iota(shape, 1), iota(shape, 0)
    rows = shape[0]
    x, z = lane >> 2, lane & 3

    def sides(v):
        return (
            down(v, 4),
            up(v, 4),
            pltpu.roll(v, 1, 0),
            pltpu.roll(v, rows - 1, 0),
            down(v, 1),
            up(v, 1),
        )

    cuts = (x == 0, x == nx - 1, row == 0, row == rows - 1, z == 0, z == 3)
    total = jnp.zeros(shape, F32)
    faces = []
    for cut, beyond in zip(cuts, sides(k)):
        value = face(k, beyond)
        faces.append(jnp.where(cut, 0.0, value))
        total = total + jnp.where(cut, k, value)
    weight = OMEGA * reciprocal(total)
    faces = [weight * value for value in faces]
    start = weight * g

    def step(_, v):
        parts = [c * beyond for c, beyond in zip(faces, sides(v))]
        return (KEEP * v + start) + ((parts[0] + parts[1]) + (parts[2] + parts[3]) + (parts[4] + parts[5]))

    return lax.fori_loop(0, COARSE_SWEEPS - 1, step, start)


N_SPLIT = 10
N_WHOLE = 7


def kernel(gx_size, gy_size, head, recharge, conductivity, out, *refs):
    refs = list(refs)
    gx, gy = lax.axis_index("gx"), lax.axis_index("gy")
    split = []
    for number, level in enumerate(SPLIT):
        nx, ny = gx_size * level.bx, gy_size * level.by
        split.append(Split(level, nx, ny, gx, gy, refs[:N_SPLIT]))
        del refs[:N_SPLIT]
    whole = []
    for number in (3, 4):
        whole.append(Whole(number, gx_size, gy_size, refs[:N_WHOLE]))
        del refs[:N_WHOLE]
    (
        res0,
        res1,
        res2,
        wide0,
        wide1,
        rows_k,
        rows_g,
        strip_k,
        strip_g,
        rest,
        coarse5,
        tally,
        local_sem,
        send_sem,
        recv_sem,
    ) = refs
    zero, one, two = split
    three, four = whole

    def device(dx, dy):
        return {
            "gx": lax.rem(gx + (dx + gx_size), gx_size),
            "gy": lax.rem(gy + (dy + gy_size), gy_size),
        }

    barrier = pltpu.get_barrier_semaphore()

    def greet(dx, dy):
        pl.semaphore_signal(
            barrier, inc=1, device_id=device(dx, dy), device_id_type=pl.DeviceIdType.MESH
        )

    local = [
        pltpu.make_async_copy(
            conductivity,
            zero.k.at[pl.ds(4, BLOCK_X), pl.ds(PAD + 4, BLOCK_Y), :],
            local_sem.at[0],
        ),
        pltpu.make_async_copy(
            head, zero.va.at[pl.ds(4, BLOCK_X), pl.ds(PAD + 4, BLOCK_Y), :], local_sem.at[1]
        ),
        pltpu.make_async_copy(
            recharge, zero.g.at[pl.ds(3, BLOCK_X), pl.ds(4, BLOCK_Y), :], local_sem.at[2]
        ),
    ]
    for copy in local:
        copy.start()

    greeted = 0
    for dx, dy, _, _ in partners(SPLIT[2], 6):
        greet(dx, dy)
        greeted += 1

    def greet_y(k, carry):
        greet(0, k)
        return carry

    def greet_x(k, carry):
        greet(k, 0)
        return carry

    if gy_size > 5:
        lax.fori_loop(3, gy_size - 2, greet_y, 0)
        greeted += gy_size - 5
    if gx_size > 3:
        lax.fori_loop(2, gx_size - 1, greet_x, 0)
        greeted += gx_size - 3

    for ref in whole:
        ref.clear_edges()
    pl.semaphore_wait(barrier, greeted)

    def push(src, dst, stage, dx, dy):
        pltpu.make_async_remote_copy(
            src_ref=src,
            dst_ref=dst,
            send_sem=send_sem.at[stage],
            recv_sem=recv_sem.at[stage],
            device_id=device(dx, dy),
            device_id_type=pl.DeviceIdType.MESH,
        ).start()

    def exchange(level, halo, stage, src, src_x, src_row, dst, dst_x, dst_row):
        for dx, dy, xs, ys in partners(level, halo):
            push(
                src.at[pl.ds(src_x + xs[0], xs[1]), pl.ds(src_row + ys[0], ys[1]), :],
                dst.at[pl.ds(dst_x + xs[2], xs[1]), pl.ds(dst_row + ys[2], ys[1]), :],
                stage,
                dx,
                dy,
            )

    def arrived(stage, rows):
        block = tally.at[pl.ds(0, rows), :]
        pltpu.make_async_copy(block, block, recv_sem.at[stage]).wait()

    def sent(stage, rows):
        block = tally.at[pl.ds(0, rows), :]
        pltpu.make_async_copy(block, block, send_sem.at[stage]).wait()

    def gather_y(strip, stage):
        def step(k, carry):
            push(strip.at[pl.ds(gy, 1), :], strip.at[pl.ds(gy, 1), :], stage, 0, k)
            return carry

        lax.fori_loop(1, gy_size, step, 0)

    def gather_x(strip, place, stage):
        def step(k, carry):
            push(strip, place, stage, k, 0)
            return carry

        lax.fori_loop(1, gx_size, step, 0)

    lv0, lv1, lv2 = SPLIT
    exchange(lv0, lv0.hk, 0, conductivity, 0, 0, zero.k, 4, PAD + 4)
    exchange(lv0, 4, 1, head, 0, 0, zero.va, 4, PAD + 4)
    exchange(lv0, lv0.hg, 2, recharge, 0, 0, zero.g, 3, 4)

    def reader(ref, x0, row0, rows):
        return lambda x, offset: ref[pl.ds(x0 + x, 1), pl.ds(row0 + offset, rows, stride=2), :]

    def writer(ref, x0, row0, rows):
        def write(x, value):
            ref[pl.ds(x0 + x, 1), pl.ds(row0, rows), :] = value

        return write

    def pack_3(rows):
        lane, row = iota((8, LANES), 1), iota((8, LANES), 0)
        picked = lane_gather(rows[...], (lane & 15) * 8)
        return jnp.sum(jnp.where((lane >> 4) == row, picked, 0.0), axis=0, keepdims=True)

    def row_writer(ref):
        def write(x, value):
            ref[pl.ds(2 * x, 2), :] = value.reshape(2, LANES)

        return write

    local[0].wait()
    restrict(reader(zero.k, 4, PAD + 4, 8), 16, 8, 1, 0.125, writer(one.k, 5, PAD + 4, 8))
    restrict(reader(one.k, 5, PAD + 4, 4), 8, 4, 2, 0.125, writer(two.k, 6, PAD + 6, 4))
    restrict(reader(two.k, 6, PAD + 6, 2), 4, 2, 4, 0.125, row_writer(rows_k))
    exchange(lv1, lv1.hk, 3, one.k, 5, PAD + 4, one.k, 5, PAD + 4)
    strip_k[pl.ds(gy, 1), :] = pack_3(rows_k)
    gather_y(strip_k, 7)
    exchange(lv2, lv2.hk, 5, two.k, 6, PAD + 6, two.k, 6, PAD + 6)

    arrived(0, exchange_rows(lv0, lv0.hk))
    zero.faces()
    arrived(7, gy_size - 1)
    inner = pl.ds(PAD, gy_size)
    three.k[pl.ds(gx + 1, 1), inner, :] = strip_k[...].reshape(1, gy_size, LANES)
    gather_x(strip_k, three.k.at[gx + 1, inner, :], 8)
    local[1].wait()
    local[2].wait()
    arrived(1, exchange_rows(lv0, 4))
    arrived(2, exchange_rows(lv0, lv0.hg))
    zero.sweep(zero.va, zero.vb, 3)
    zero.sweep(zero.vb, zero.va, 2)
    zero.residual(zero.va, res0)
    restrict(reader(res0, 0, 0, 8), 16, 8, 1, 0.5, writer(one.g, 4, 4, 8))

    exchange(lv1, lv1.hg, 4, one.g, 4, 4, one.g, 4, 4)
    arrived(3, exchange_rows(lv1, lv1.hk))
    one.faces()
    arrived(4, exchange_rows(lv1, lv1.hg))
    one.first_sweep(one.va)
    one.sweep(one.va, one.vb, 3)
    one.residual(one.vb, res1)
    restrict(reader(res1, 0, 0, 4), 8, 4, 2, 0.5, writer(two.g, 5, 6, 4))

    exchange(lv2, lv2.hg, 6, two.g, 5, 6, two.g, 5, 6)
    arrived(5, exchange_rows(lv2, lv2.hk))
    two.faces()
    arrived(6, exchange_rows(lv2, lv2.hg))
    two.first_sweep(two.va)
    two.sweep(two.va, two.vb, 4)
    two.residual(two.vb, res2)
    restrict(reader(res2, 0, 0, 2), 4, 2, 4, 0.5, row_writer(rows_g))

    strip_g[pl.ds(gy, 1), :] = pack_3(rows_g)
    gather_y(strip_g, 9)
    arrived(8, (gx_size - 1) * gy_size)
    three.faces()

    def coarser_k(i, carry):
        four.k[pl.ds(i + 1, 1), inner, :] = 0.125 * octet_3(three.k[pl.ds(i + 1, 1), inner, :])
        return carry

    lax.fori_loop(0, gx_size, coarser_k, 0, unroll=4)
    rest[...] = four.k[pl.ds(1, gx_size), inner, :]
    k5 = pack_5(rest, 1.0, 0.125, gx_size, gy_size)
    four.faces()
    arrived(9, gy_size - 1)
    three.g[pl.ds(gx, 1)] = strip_g[...].reshape(1, gy_size, LANES)
    gather_x(strip_g, three.g.at[gx], 10)
    arrived(10, (gx_size - 1) * gy_size)

    three.first_sweep(three.va)
    three.sweep(three.va, three.vb)

    def to_four(i, value):
        four.g[pl.ds(i, 1)] = 0.5 * octet_3(value)

    three.residual(three.vb, to_four)
    four.first_sweep(four.va)
    four.sweep(four.va, four.vb)

    def to_five(i, value):
        rest[pl.ds(i, 1)] = value

    four.residual(four.vb, to_five)
    v5 = solve_5(k5, pack_5(rest, 0.0, 0.5, gx_size, gy_size), gx_size)

    coarse5[pl.ds(0, gy_size // 2, stride=2), :] = v5
    coarse5[pl.ds(1, gy_size // 2, stride=2), :] = v5
    wide5 = coarse5[...]

    def from_five(i):
        index = i * 4 + ((iota((gy_size, LANES), 1) & 15) >> 2)
        return lane_gather(wide5, index).reshape(1, gy_size, LANES)

    four.correct(four.vb, from_five)
    four.sweep(four.vb, four.va)
    four.sweep(four.va, four.vb)
    three.correct(three.vb, lambda i: four.vb[pl.ds(i + 1, 1), inner, :])
    three.sweep(three.vb, three.va)
    three.sweep(three.va, three.vb)

    row = iota((lv2.rows, LANES), 0)
    lane = iota((lv2.rows, LANES), 1)
    y3 = (row >> 1) - 1
    for dx in (-1, 0, 1):
        gxn = lax.rem(gx + (dx + gx_size), gx_size) + 1
        near = []
        for dy in (-1, 0, 1):
            gyn = lax.rem(gy + (dy + gy_size), gy_size) + PAD
            near.append(three.vb[pl.ds(gxn, 1), pl.ds(gyn, 1), :].reshape(1, LANES))
        rows = jnp.where(y3 < 2, near[0], jnp.where(y3 < 4, near[1], near[2]))
        for x in ((2, 3), (0, 1, 2, 3), (0, 1))[dx + 1]:
            copies = lane_gather(rows, (2 * x + (y3 & 1)) * 16 + (lane >> 3))
            for child in range(2):
                place = (2 * (4 * dx + x) + child + 6, pl.ds(PAD, lv2.rows))
                two.vb[place] = two.vb[place] + copies
    two.sweep(two.vb, two.va, 3)
    two.sweep(two.va, two.vb, 2)

    def coarse_rows(ref, x0):
        return lambda j, row0, rows: ref[pl.ds(x0 + j, 1), pl.ds(PAD + row0, rows), :]

    one.correct(one.vb, coarse_rows(two.vb, 6 - 2), -2, 12, 5, 4, wide1)
    one.sweep(one.vb, one.va, 2)
    one.sweep(one.va, one.vb, 1)
    zero.correct(zero.va, coarse_rows(one.vb, 5 - 1), -1, 18, 4, 2, wide0)
    zero.sweep(zero.va, zero.vb, 1)
    zero.last_sweep(zero.vb, out)

    sent(0, exchange_rows(lv0, lv0.hk))
    sent(1, exchange_rows(lv0, 4))
    sent(2, exchange_rows(lv0, lv0.hg))
    sent(3, exchange_rows(lv1, lv1.hk))
    sent(4, exchange_rows(lv1, lv1.hg))
    sent(5, exchange_rows(lv2, lv2.hk))
    sent(6, exchange_rows(lv2, lv2.hg))
    sent(7, gy_size - 1)
    sent(8, (gx_size - 1) * gy_size)
    sent(9, gy_size - 1)
    sent(10, (gx_size - 1) * gy_size)


def on_device(gx_size, gy_size, head, recharge, conductivity):
    scratch = []
    for level in SPLIT:
        scratch += Split.scratch(level)
    for _ in range(2):
        scratch += Whole.scratch(gx_size, gy_size)
    scratch += [
        pltpu.VMEM((32, 16, LANES), F32),
        pltpu.VMEM((16, 8, LANES), F32),
        pltpu.VMEM((8, 4, LANES), F32),
        pltpu.VMEM((18, 24, LANES), F32),
        pltpu.VMEM((12, 16, LANES), F32),
        pltpu.VMEM((8, LANES), F32),
        pltpu.VMEM((8, LANES), F32),
        pltpu.VMEM((gy_size, LANES), F32),
        pltpu.VMEM((gy_size, LANES), F32),
        pltpu.VMEM((gx_size, gy_size, LANES), F32),
        pltpu.VMEM((gy_size, LANES), F32),
        pltpu.VMEM((TALLY_ROWS, LANES), F32),
        pltpu.SemaphoreType.DMA((3,)),
        pltpu.SemaphoreType.DMA((11,)),
        pltpu.SemaphoreType.DMA((11,)),
    ]

    def body(*refs):
        kernel(gx_size, gy_size, *refs)

    return pl.pallas_call(
        body,
        out_shape=jax.ShapeDtypeStruct(head.shape, F32),
        in_specs=[pl.BlockSpec(memory_space=pl.ANY)] * 3,
        out_specs=pl.BlockSpec(memory_space=pltpu.VMEM),
        scratch_shapes=scratch,
        compiler_params=pltpu.CompilerParams(
            collective_id=0, has_side_effects=True, vmem_limit_bytes=40 * 1024 * 1024
        ),
        name="vcycle",
    )(head, recharge, conductivity)


def solution(mesh):
    gx_size, gy_size = mesh.shape["gx"], mesh.shape["gy"]

    def one_device(head, recharge, conductivity):
        return on_device(gx_size, gy_size, head, recharge, conductivity)

    spec = P("gx", "gy", None)
    return jax.shard_map(
        one_device, mesh=mesh, in_specs=(spec, spec, spec), out_specs=spec, check_vma=False
    )
```

time: 597 us -> 63 us (0.11); the launches traced: 585 us -> 62.9 us
  starting transfers between devices: 308 us -> 0 us
  blocking collectives: 105 us -> 0 us
  local copies, waits for them, and re-layouts: 74.5 us -> 3.55 us
  waiting for transfers between devices: 65.5 us -> 0 us
  Pallas kernels: 0 us -> 59.3 us
  other arithmetic: 30.5 us -> 0 us
    ppermute x94 -> x0, starting transfers between devices: 308 us -> none  [the longest x47 221 us: extended(): lax.ppermute(lax.slice_in_dim(block, block.shape[dim] - width, None, axis...]
    all_gather x4 -> x0, blocking collectives: 105 us -> none  [the longest x1 31.7 us: descend(): lax.all_gather(source, 'gy', axis=1, tiled=True)]
    ppermute x94 -> x0, waiting for transfers between devices: 65.5 us -> none  [the longest x47 47.2 us: extended(): lax.ppermute(lax.slice_in_dim(block, 0, width, axis=dim), axis, backward)]
    pallas_call x0 -> x1, Pallas kernels: none -> 59.3 us  [on_device(): pl.pallas_call(body, out_shape=jax.ShapeDtypeStruct(head.shape, F32), in_...]
    reshape x7 -> x0, local copies, waits for them, and re-layouts: 56.5 us -> none  [the longest x4 40.5 us: restrict(): return field.reshape(a // 2, 2, b // 2, 2, c // 2, 2).mean(axis=(1, 3, 5))]
    reduce_sum x14 -> x0, other arithmetic: 18.5 us -> none  [restrict(): return field.reshape(a // 2, 2, b // 2, 2, c // 2, 2).mean(axis=(1, 3, 5))]
    broadcast_in_dim x8 -> x0, local copies, waits for them, and re-layouts: 8.62 us -> none  [prolong(): jnp.broadcast_to(field[:, None, :, None, :, None], (a, 2, b, 2, c, 2))]
  transfers between devices with their start and end apart: 94 -> 0, of which waited for: 40 -> 0; matrix products, arithmetic and copies ran while one was open for 12% -> 0% of each run, Pallas kernels for 0% -> 0%
where the time goes in v1:
time: 63 us; the launch traced here: 62.9 us
  Pallas kernels  59.3 us (94%)
  local copies, waits for them, and re-layouts  3.55 us (6%)
    pallas_call x1, Pallas kernels, on_device(): pl.pallas_call(body, out_shape=jax.ShapeDtypeStruct(head.shape, F32), in_...  59.3 us
    unnamed x7, local copies, waits for them, and re-layouts  3.55 us

profile of v1, /device:TPU:1, one launch (start us, length us, event | category | flops | bytes accessed | tf_op | source)
XLA Modules:
  0.0 62.9 jit_solution(14769686560551786825)
XLA Ops:
  0.0 0.0 copy-start
  0.0 0.9 %copy-done = f32[32,16,128]{2,1,0:T(8,128)S(1)} copy-done((f32[32,16,128]{2,1,0:T(8,128)S(1)}, f32[32,16,128]{2,1,0:T(8,128)}, u32[]{:S(2)}) %copy-start) | copy-done | bytes 262168
  1.0 0.0 copy-start.1
  1.0 0.9 %copy-done.1 = f32[32,16,128]{2,1,0:T(8,128)S(1)} copy-done((f32[32,16,128]{2,1,0:T(8,128)S(1)}, f32[32,16,128]{2,1,0:T(8,128)}, u32[]{:S(2)}) %copy-start.1) | copy-done | bytes 262168
  1.9 0.0 copy-start.2
  1.9 0.9 %copy-done.2 = f32[32,16,128]{2,1,0:T(8,128)S(1)} copy-done((f32[32,16,128]{2,1,0:T(8,128)S(1)}, f32[32,16,128]{2,1,0:T(8,128)}, u32[]{:S(2)}) %copy-start.2) | copy-done | bytes 262168
  2.9 59.3 %vcycle.1 = f32[32,16,128]{2,1,0:T(8,128)S(1)} custom-call(f32[32,16,128]{2,1,0:T(8,128)S(1)} %copy-done, f32[32,16,128]{2,1,0:T(8,128)S(1)} %copy-done.1, f32[32,16,128]{2,1,0:T(8,128)S(1)} %copy-done.2), custom_call_target="tpu_custom_call" | custom-call | tf_op jit(solution)/shard_map/vcycle/pallas_call | solution.py:729
  62.2 0.7 %copy.5 = f32[32,16,128]{2,1,0:T(8,128)} copy(f32[32,16,128]{2,1,0:T(8,128)S(1)} %vcycle.1) | data formatting | bytes 524288
Async XLA Ops:
  0.0 0.9 %copy-start = (f32[32,16,128]{2,1,0:T(8,128)S(1)}, f32[32,16,128]{2,1,0:T(8,128)}, u32[]{:S(2)}) copy-start(f32[32,16,128]{2,1,0:T(8,128)} %refs_0_.1) | copy-start | bytes 786436
  1.0 0.9 %copy-start.1 = (f32[32,16,128]{2,1,0:T(8,128)S(1)}, f32[32,16,128]{2,1,0:T(8,128)}, u32[]{:S(2)}) copy-start(f32[32,16,128]{2,1,0:T(8,128)} %refs_1_.1) | copy-start | bytes 786436
  1.9 0.9 %copy-start.2 = (f32[32,16,128]{2,1,0:T(8,128)S(1)}, f32[32,16,128]{2,1,0:T(8,128)}, u32[]{:S(2)}) copy-start(f32[32,16,128]{2,1,0:T(8,128)} %refs_2_.1) | copy-start | bytes 786436

commit v2 on v1

v2 whole, which is shorter than its diff:
```python
from typing import NamedTuple

import jax
import jax.numpy as jnp
from jax import lax
from jax.experimental import pallas as pl
from jax.experimental.pallas import tpu as pltpu
from jax.sharding import PartitionSpec as P

F32 = jnp.float32
LANES = 128
PAD = 8
OMEGA = 0.8
KEEP = 1.0 - OMEGA
COARSE_SWEEPS = 16
BLOCK_X = 32
BLOCK_Y = 16
TALLY_ROWS = 512

class Level(NamedTuple):
    bx: int
    by: int
    hx: int
    rows: int
    first: int
    span: int
    reach: int
    hk: int
    hg: int
    cyrows: int


SPLIT = (
    Level(32, 16, 3, 24, 4, 1, 1, 4, 3, 24),
    Level(16, 8, 4, 16, 4, 2, 1, 5, 4, 24),
    Level(8, 4, 5, 16, 6, 4, 2, 6, 5, 16),
)


def reciprocal(x):
    guess = pltpu.reciprocal(x, approx=True)
    return guess * (2.0 - x * guess)


def face(a, b):
    return (2.0 * a * b) * reciprocal(a + b)


def iota(shape, dim):
    return lax.broadcasted_iota(jnp.int32, shape, dim)


def flag(condition):
    return jnp.where(condition, 1.0, 0.0).astype(F32)


def up(value, shift):
    return pltpu.roll(value, LANES - shift, value.ndim - 1)


def down(value, shift):
    return pltpu.roll(value, shift, value.ndim - 1)


def swap(value, bit):
    if 2 * bit == LANES:
        return down(value, bit)
    lane = iota(value.shape, value.ndim - 1)
    return jnp.where((lane & bit) == 0, up(value, bit), down(value, bit))


def lane_gather(value, index):
    return jnp.take_along_axis(value, index, axis=1)


def segment(step, block, halo):
    low = max(0, step * block - halo)
    high = min(block, (step + 1) * block + halo)
    return low, high - low, low - step * block


def partners(level, halo):
    for dx in (-1, 0, 1):
        for dy in range(-level.reach, level.reach + 1):
            if (dx, dy) != (0, 0):
                yield dx, dy, segment(dx, level.bx, halo), segment(dy, level.by, halo)


def exchange_rows(level, halo):
    return sum(xs[1] * ys[1] for _, _, xs, ys in partners(level, halo))


class Split:
    def __init__(self, level, nx, ny, gx, gy, refs):
        self.at = level
        self.nx, self.ny, self.gx, self.gy = nx, ny, gx, gy
        (self.k, self.va, self.vb, self.g, self.cx, self.cy, self.czl, self.czh, self.w, self.d) = refs

    @staticmethod
    def scratch(level):
        x, rows = level.bx + 2 * level.hx, level.rows
        padded = pltpu.VMEM((x + 2, rows + 2 * PAD, LANES), F32)
        plain = pltpu.VMEM((x, rows, LANES), F32)
        return [
            padded,
            padded,
            padded,
            plain,
            pltpu.VMEM((x + 1, rows, LANES), F32),
            pltpu.VMEM((x, rows + PAD, LANES), F32),
            plain,
            plain,
            plain,
            plain,
        ]

    def faces(self):
        lv = self.at
        count, rows, span = lv.bx + 2 * lv.hx, lv.rows, lv.span
        y = self.gy * lv.by + iota((1, lv.cyrows, LANES), 1) - lv.first
        y_open = flag((y != 0) & (y != self.ny))
        y = y[:, :rows]
        lane = iota((1, rows, LANES), 2)
        z_open = flag(lane >= span)
        cuts = flag((y == 0) | (y == self.ny)) + flag((y == -1) | (y == self.ny - 1))
        cuts = cuts + flag(lane < span) + flag(lane >= LANES - span)
        inner = pl.ds(PAD, rows)
        all_x = pl.ds(1, count)
        here = self.k[all_x, inner, :]
        self.cx[...] = face(
            self.k[pl.ds(0, count + 1), inner, :], self.k[pl.ds(1, count + 1), inner, :]
        )
        cut_low, cut_high = flag(self.gx == 0), flag(self.gx * lv.bx + lv.bx == self.nx)
        for i, cut in ((lv.hx, cut_low), (lv.hx + lv.bx, cut_high)):
            self.cx[i] = self.cx[i] * (1.0 - cut)
        self.cy[:, pl.ds(0, lv.cyrows), :] = y_open * face(
            self.k[all_x, pl.ds(PAD - 1, lv.cyrows), :], self.k[all_x, pl.ds(PAD, lv.cyrows), :]
        )
        low_z = face(down(here, span), here) * z_open
        high_z = up(low_z, span)
        self.czl[...] = low_z
        self.czh[...] = high_z
        total = self.cx[pl.ds(0, count)] + self.cx[pl.ds(1, count)]
        total = total + (self.cy[:, pl.ds(0, rows), :] + self.cy[:, pl.ds(1, rows), :])
        self.d[...] = (total + (low_z + high_z)) + here * cuts
        for i, cut in ((lv.hx, cut_low), (lv.hx + lv.bx - 1, cut_high)):
            self.d[i] = self.d[i] + self.k[i + 1, inner, :] * cut
        self.w[...] = OMEGA * reciprocal(self.d[...])

    def beside(self, v, low, count, row, rows):
        span = self.at.span
        inner, own = pl.ds(PAD + row, rows), pl.ds(row, rows)
        x, mid = pl.ds(low, count), pl.ds(low + 1, count)
        here = v[mid, inner, :]
        along_x = self.cx[x, own, :] * v[x, inner, :] + self.cx[mid, own, :] * v[pl.ds(low + 2, count), inner, :]
        along_y = (
            self.cy[x, own, :] * v[mid, pl.ds(PAD + row - 1, rows), :]
            + self.cy[x, pl.ds(row + 1, rows), :] * v[mid, pl.ds(PAD + row + 1, rows), :]
        )
        along_z = self.czl[x, own, :] * down(here, span) + self.czh[x, own, :] * up(here, span)
        return here, (along_x + along_y) + along_z

    def first_sweep(self, dst):
        dst[pl.ds(1, self.at.bx + 2 * self.at.hx), pl.ds(PAD, self.at.rows), :] = self.w[...] * self.g[...]

    def sweep(self, src, dst, halo):
        lv = self.at
        low, count = lv.hx - halo, lv.bx + 2 * halo
        here, total = self.beside(src, low, count, 0, lv.rows)
        x = pl.ds(low, count)
        dst[pl.ds(low + 1, count), pl.ds(PAD, lv.rows), :] = KEEP * here + self.w[x] * (self.g[x] + total)

    def last_sweep(self, src, out):
        lv = self.at
        x, own = pl.ds(lv.hx, lv.bx), pl.ds(lv.first, lv.by)
        here, total = self.beside(src, lv.hx, lv.bx, lv.first, lv.by)
        out[...] = KEEP * here + self.w[x, own, :] * (self.g[x, own, :] + total)

    def residual(self, v):
        lv = self.at
        x, own = pl.ds(lv.hx, lv.bx), pl.ds(lv.first, lv.by)
        here, total = self.beside(v, lv.hx, lv.bx, lv.first, lv.by)
        return self.g[x, own, :] + total - self.d[x, own, :] * here

    def correct(self, v, coarse, x0, count, wide):
        rows = self.at.rows
        half = rows // 2
        wide[:, pl.ds(0, half, stride=2), :] = coarse
        wide[:, pl.ds(1, half, stride=2), :] = coarse
        place = (pl.ds(x0, 2 * count), pl.ds(PAD, rows))
        copies = jnp.broadcast_to(wide[...][:, None], (count, 2, rows, LANES))
        v[place] = v[place] + copies.reshape(2 * count, rows, LANES)


def restrict(value, half, span, scale):
    x, y, _ = value.shape
    value = value.reshape(x // 2, 2, y, LANES)
    half[...] = value[:, 0] + value[:, 1]
    total = half[:, pl.ds(0, y // 2, stride=2), :] + half[:, pl.ds(1, y // 2, stride=2), :]
    return scale * (total + swap(total, span))


class Whole:
    def __init__(self, number, nx, ny, refs):
        self.number, self.nx, self.ny = number, nx, ny
        self.k, self.va, self.vb, self.g, self.c, self.w, self.d = refs

    @staticmethod
    def scratch(nx, ny):
        padded = pltpu.VMEM((nx + 2, ny + 2 * PAD, LANES), F32)
        plain = pltpu.VMEM((nx, ny, LANES), F32)
        return [padded, padded, padded, plain, pltpu.VMEM((6, nx, ny, LANES), F32), plain, plain]

    def clear_edges(self):
        for ref in (self.k, self.va, self.vb):
            for x in (0, self.nx + 1):
                ref[x] = jnp.zeros((self.ny + 2 * PAD, LANES), F32)
            for row in (0, PAD + self.ny):
                ref[:, pl.ds(row, PAD), :] = jnp.zeros((self.nx + 2, PAD, LANES), F32)

    def inside(self, ref):
        return ref.at[pl.ds(1, self.nx), pl.ds(PAD, self.ny), :]

    def neighbours(self, v):
        inner, all_x = pl.ds(PAD, self.ny), pl.ds(1, self.nx)
        here = v[all_x, inner, :]
        before = v[pl.ds(0, self.nx), inner, :]
        after = v[pl.ds(2, self.nx), inner, :]
        under = v[all_x, pl.ds(PAD - 1, self.ny), :]
        over = v[all_x, pl.ds(PAD + 1, self.ny), :]
        lane = iota((1, self.ny, LANES), 2)
        if self.number == 3:
            before = down(jnp.where(lane >= 96, before, here), 32)
            after = up(jnp.where(lane < 32, after, here), 32)
            odd = (lane & 16) != 0
            under = swap(jnp.where(odd, under, here), 16)
            over = swap(jnp.where(odd, here, over), 16)
            span = 1
        else:
            before = down(jnp.where(lane >= 64, before, here), 64)
            after = up(jnp.where(lane < 64, after, here), 64)
            span = 2
        return (before, after, under, over, down(here, span), up(here, span)), here

    def faces(self):
        shape = (self.nx, self.ny, LANES)
        lane, row, x = iota(shape, 2), iota(shape, 1), iota(shape, 0)
        z = lane & 15
        if self.number == 3:
            first_x, last_x, first_y, last_y = lane < 32, lane >= 96, (lane & 16) == 0, (lane & 16) != 0
            first_z, last_z = z == 0, z == 15
            first_y, last_y = (row == 0) & first_y, (row == self.ny - 1) & last_y
        else:
            first_x, last_x, first_y, last_y = lane < 64, lane >= 64, row == 0, row == self.ny - 1
            first_z, last_z = z < 2, z >= 14
        first_x, last_x = (x == 0) & first_x, (x == self.nx - 1) & last_x
        sides, here = self.neighbours(self.k)
        total = jnp.zeros(shape, F32)
        for n, cut in enumerate((first_x, last_x, first_y, last_y, first_z, last_z)):
            value = face(here, sides[n])
            self.c[n] = jnp.where(cut, 0.0, value)
            total = total + jnp.where(cut, here, value)
        self.d[...] = total
        self.w[...] = OMEGA * reciprocal(total)

    def beside(self, v):
        sides, here = self.neighbours(v)
        parts = [self.c[n] * sides[n] for n in range(6)]
        return here, (parts[0] + parts[1]) + (parts[2] + parts[3]) + (parts[4] + parts[5])

    def first_sweep(self, dst):
        self.inside(dst)[...] = self.w[...] * self.g[...]

    def sweep(self, src, dst):
        here, total = self.beside(src)
        self.inside(dst)[...] = KEEP * here + self.w[...] * (self.g[...] + total)

    def residual(self, v):
        here, total = self.beside(v)
        return self.g[...] + total - self.d[...] * here

    def correct(self, v, values):
        place = self.inside(v)
        place[...] = place[...] + values


def octet_3(value):
    value = value + swap(value, 1)
    value = value + swap(value, 16)
    return value + swap(value, 32)


def pack_5(ref, fill, scale, nx, ny):
    half = ny // 2
    shape = (nx, half, LANES)
    rows = ref[:, pl.ds(0, half, stride=2), :] + ref[:, pl.ds(1, half, stride=2), :]
    rows = rows + swap(rows, 2)
    rows = scale * (rows + swap(rows, 64))
    index = (iota((nx * half, LANES), 1) & 3) * 4
    rows = lane_gather(rows.reshape(nx * half, LANES), index).reshape(shape)
    packed = jnp.sum(jnp.where((iota(shape, 2) >> 2) == iota(shape, 0), rows, 0.0), axis=0)
    return packed + jnp.where(iota((half, LANES), 1) >= 4 * nx, fill, 0.0)


def faces_5(k, nx):
    shape = k.shape
    lane, row = iota(shape, 1), iota(shape, 0)
    x, z = lane >> 2, lane & 3
    cuts = (x == 0, x == nx - 1, row == 0, row == shape[0] - 1, z == 0, z == 3)
    total = jnp.zeros(shape, F32)
    faces = []
    for cut, beyond in zip(cuts, sides_5(k)):
        value = face(k, beyond)
        faces.append(jnp.where(cut, 0.0, value))
        total = total + jnp.where(cut, k, value)
    weight = OMEGA * reciprocal(total)
    return weight, [weight * value for value in faces]


def sides_5(v):
    rows = v.shape[0]
    return (down(v, 4), up(v, 4), pltpu.roll(v, 1, 0), pltpu.roll(v, rows - 1, 0), down(v, 1), up(v, 1))


def solve_5(weight, faces, g):
    start = weight * g

    def step(_, v):
        parts = [c * beyond for c, beyond in zip(faces, sides_5(v))]
        return (KEEP * v + start) + ((parts[0] + parts[1]) + (parts[2] + parts[3]) + (parts[4] + parts[5]))

    return lax.fori_loop(0, COARSE_SWEEPS - 1, step, start)


N_SPLIT = 10
N_WHOLE = 7


def kernel(gx_size, gy_size, head, recharge, conductivity, out, *refs):
    refs = list(refs)
    gx, gy = lax.axis_index("gx"), lax.axis_index("gy")
    split = []
    for number, level in enumerate(SPLIT):
        nx, ny = gx_size * level.bx, gy_size * level.by
        split.append(Split(level, nx, ny, gx, gy, refs[:N_SPLIT]))
        del refs[:N_SPLIT]
    whole = []
    for number in (3, 4):
        whole.append(Whole(number, gx_size, gy_size, refs[:N_WHOLE]))
        del refs[:N_WHOLE]
    (
        half0,
        half1,
        half2,
        wide0,
        wide1,
        rows_k,
        rows_g,
        strip_k,
        strip_g,
        rest,
        coarse5,
        tally,
        local_sem,
        send_sem,
        recv_sem,
    ) = refs
    zero, one, two = split
    three, four = whole

    def device(dx, dy):
        return {
            "gx": lax.rem(gx + (dx + gx_size), gx_size),
            "gy": lax.rem(gy + (dy + gy_size), gy_size),
        }

    barrier = pltpu.get_barrier_semaphore()

    def greet(dx, dy):
        pl.semaphore_signal(
            barrier, inc=1, device_id=device(dx, dy), device_id_type=pl.DeviceIdType.MESH
        )

    local = [
        pltpu.make_async_copy(
            conductivity,
            zero.k.at[pl.ds(4, BLOCK_X), pl.ds(PAD + 4, BLOCK_Y), :],
            local_sem.at[0],
        ),
        pltpu.make_async_copy(
            head, zero.va.at[pl.ds(4, BLOCK_X), pl.ds(PAD + 4, BLOCK_Y), :], local_sem.at[1]
        ),
        pltpu.make_async_copy(
            recharge, zero.g.at[pl.ds(3, BLOCK_X), pl.ds(4, BLOCK_Y), :], local_sem.at[2]
        ),
    ]
    for copy in local:
        copy.start()

    greeted = 0
    for dx, dy, _, _ in partners(SPLIT[2], 6):
        greet(dx, dy)
        greeted += 1

    def greet_y(k, carry):
        greet(0, k)
        return carry

    def greet_x(k, carry):
        greet(k, 0)
        return carry

    if gy_size > 5:
        lax.fori_loop(3, gy_size - 2, greet_y, 0)
        greeted += gy_size - 5
    if gx_size > 3:
        lax.fori_loop(2, gx_size - 1, greet_x, 0)
        greeted += gx_size - 3

    for ref in whole:
        ref.clear_edges()
    pl.semaphore_wait(barrier, greeted)

    def push(src, dst, stage, dx, dy):
        pltpu.make_async_remote_copy(
            src_ref=src,
            dst_ref=dst,
            send_sem=send_sem.at[stage],
            recv_sem=recv_sem.at[stage],
            device_id=device(dx, dy),
            device_id_type=pl.DeviceIdType.MESH,
        ).start()

    def exchange(level, halo, stage, src, src_x, src_row, dst, dst_x, dst_row):
        for dx, dy, xs, ys in partners(level, halo):
            push(
                src.at[pl.ds(src_x + xs[0], xs[1]), pl.ds(src_row + ys[0], ys[1]), :],
                dst.at[pl.ds(dst_x + xs[2], xs[1]), pl.ds(dst_row + ys[2], ys[1]), :],
                stage,
                dx,
                dy,
            )

    def arrived(stage, rows):
        block = tally.at[pl.ds(0, rows), :]
        pltpu.make_async_copy(block, block, recv_sem.at[stage]).wait()

    def sent(stage, rows):
        block = tally.at[pl.ds(0, rows), :]
        pltpu.make_async_copy(block, block, send_sem.at[stage]).wait()

    def gather_y(strip, stage):
        def step(k, carry):
            push(strip.at[pl.ds(gy, 1), :], strip.at[pl.ds(gy, 1), :], stage, 0, k)
            return carry

        lax.fori_loop(1, gy_size, step, 0)

    def gather_x(strip, place, stage):
        def step(k, carry):
            push(strip, place, stage, k, 0)
            return carry

        lax.fori_loop(1, gx_size, step, 0)

    lv0, lv1, lv2 = SPLIT
    exchange(lv0, lv0.hk, 0, conductivity, 0, 0, zero.k, 4, PAD + 4)
    exchange(lv0, 4, 1, head, 0, 0, zero.va, 4, PAD + 4)
    exchange(lv0, lv0.hg, 2, recharge, 0, 0, zero.g, 3, 4)

    def pack_3(rows):
        lane, row = iota((8, LANES), 1), iota((8, LANES), 0)
        picked = lane_gather(rows[...], (lane & 15) * 8)
        return jnp.sum(jnp.where((lane >> 4) == row, picked, 0.0), axis=0, keepdims=True)

    def to_rows(value, ref):
        for x in range(4):
            ref[pl.ds(2 * x, 2), :] = value[x]

    local[0].wait()
    own0 = (pl.ds(4, BLOCK_X), pl.ds(PAD + 4, BLOCK_Y))
    own1, own2 = (pl.ds(5, 16), pl.ds(PAD + 4, 8)), (pl.ds(6, 8), pl.ds(PAD + 6, 4))
    one.k[own1] = restrict(zero.k[own0], half0, 1, 0.125)
    two.k[own2] = restrict(one.k[own1], half1, 2, 0.125)
    to_rows(restrict(two.k[own2], half2, 4, 0.125), rows_k)
    strip_k[pl.ds(gy, 1), :] = pack_3(rows_k)
    exchange(lv1, lv1.hk, 3, one.k, 5, PAD + 4, one.k, 5, PAD + 4)
    gather_y(strip_k, 7)
    exchange(lv2, lv2.hk, 5, two.k, 6, PAD + 6, two.k, 6, PAD + 6)

    arrived(0, exchange_rows(lv0, lv0.hk))
    zero.faces()
    arrived(7, gy_size - 1)
    inner = pl.ds(PAD, gy_size)
    three.k[pl.ds(gx + 1, 1), inner, :] = strip_k[...].reshape(1, gy_size, LANES)
    gather_x(strip_k, three.k.at[gx + 1, inner, :], 8)
    local[1].wait()
    local[2].wait()
    arrived(1, exchange_rows(lv0, 4))
    arrived(2, exchange_rows(lv0, lv0.hg))
    zero.sweep(zero.va, zero.vb, 3)
    zero.sweep(zero.vb, zero.va, 2)
    one.g[pl.ds(4, 16), pl.ds(4, 8), :] = restrict(zero.residual(zero.va), half0, 1, 0.5)

    exchange(lv1, lv1.hg, 4, one.g, 4, 4, one.g, 4, 4)
    arrived(3, exchange_rows(lv1, lv1.hk))
    one.faces()
    arrived(4, exchange_rows(lv1, lv1.hg))
    one.first_sweep(one.va)
    one.sweep(one.va, one.vb, 3)
    two.g[pl.ds(5, 8), pl.ds(6, 4), :] = restrict(one.residual(one.vb), half1, 2, 0.5)

    exchange(lv2, lv2.hg, 6, two.g, 5, 6, two.g, 5, 6)
    arrived(5, exchange_rows(lv2, lv2.hk))
    two.faces()
    arrived(6, exchange_rows(lv2, lv2.hg))
    two.first_sweep(two.va)
    two.sweep(two.va, two.vb, 4)
    to_rows(restrict(two.residual(two.vb), half2, 4, 0.5), rows_g)
    strip_g[pl.ds(gy, 1), :] = pack_3(rows_g)

    gather_y(strip_g, 9)
    arrived(8, (gx_size - 1) * gy_size)
    three.faces()
    k4 = 0.125 * octet_3(three.inside(three.k)[...])
    four.inside(four.k)[...] = k4
    rest[...] = k4
    weight5, faces5 = faces_5(pack_5(rest, 1.0, 0.125, gx_size, gy_size), gx_size)
    four.faces()
    arrived(9, gy_size - 1)
    three.g[pl.ds(gx, 1)] = strip_g[...].reshape(1, gy_size, LANES)
    gather_x(strip_g, three.g.at[gx], 10)
    arrived(10, (gx_size - 1) * gy_size)

    three.first_sweep(three.va)
    three.sweep(three.va, three.vb)
    four.g[...] = 0.5 * octet_3(three.residual(three.vb))
    four.first_sweep(four.va)
    four.sweep(four.va, four.vb)
    rest[...] = four.residual(four.vb)
    v5 = solve_5(weight5, faces5, pack_5(rest, 0.0, 0.5, gx_size, gy_size))

    coarse5[pl.ds(0, gy_size // 2, stride=2), :] = v5
    coarse5[pl.ds(1, gy_size // 2, stride=2), :] = v5
    shape = (gx_size, gy_size, LANES)
    flat = (gx_size * gy_size, LANES)
    index = iota(shape, 0) * 4 + ((iota(shape, 2) & 15) >> 2)
    wide5 = jnp.broadcast_to(coarse5[...][None], shape).reshape(flat)
    four.correct(four.vb, lane_gather(wide5, index.reshape(flat)).reshape(shape))
    four.sweep(four.vb, four.va)
    four.sweep(four.va, four.vb)
    three.correct(three.vb, four.inside(four.vb)[...])
    three.sweep(three.vb, three.va)
    three.sweep(three.va, three.vb)

    row = iota((lv2.rows, LANES), 0)
    lane = iota((lv2.rows, LANES), 1)
    y3 = (row >> 1) - 1
    for dx in (-1, 0, 1):
        gxn = lax.rem(gx + (dx + gx_size), gx_size) + 1
        near = []
        for dy in (-1, 0, 1):
            gyn = lax.rem(gy + (dy + gy_size), gy_size) + PAD
            near.append(three.vb[pl.ds(gxn, 1), pl.ds(gyn, 1), :].reshape(1, LANES))
        rows = jnp.where(y3 < 2, near[0], jnp.where(y3 < 4, near[1], near[2]))
        for x in ((2, 3), (0, 1, 2, 3), (0, 1))[dx + 1]:
            copies = lane_gather(rows, (2 * x + (y3 & 1)) * 16 + (lane >> 3))
            for child in range(2):
                place = (2 * (4 * dx + x) + child + 6, pl.ds(PAD, lv2.rows))
                two.vb[place] = two.vb[place] + copies
    two.sweep(two.vb, two.va, 3)
    two.sweep(two.va, two.vb, 2)

    one.correct(one.vb, two.vb[pl.ds(4, 12), pl.ds(PAD + 4, 8), :], 1, 12, wide1)
    one.sweep(one.vb, one.va, 2)
    one.sweep(one.va, one.vb, 1)
    zero.correct(zero.va, one.vb[pl.ds(4, 18), pl.ds(PAD + 2, 12), :], 2, 18, wide0)
    zero.sweep(zero.va, zero.vb, 1)
    zero.last_sweep(zero.vb, out)

    sent(0, exchange_rows(lv0, lv0.hk))
    sent(1, exchange_rows(lv0, 4))
    sent(2, exchange_rows(lv0, lv0.hg))
    sent(3, exchange_rows(lv1, lv1.hk))
    sent(4, exchange_rows(lv1, lv1.hg))
    sent(5, exchange_rows(lv2, lv2.hk))
    sent(6, exchange_rows(lv2, lv2.hg))
    sent(7, gy_size - 1)
    sent(8, (gx_size - 1) * gy_size)
    sent(9, gy_size - 1)
    sent(10, (gx_size - 1) * gy_size)


def on_device(gx_size, gy_size, head, recharge, conductivity):
    scratch = []
    for level in SPLIT:
        scratch += Split.scratch(level)
    for _ in range(2):
        scratch += Whole.scratch(gx_size, gy_size)
    scratch += [
        pltpu.VMEM((16, 16, LANES), F32),
        pltpu.VMEM((8, 8, LANES), F32),
        pltpu.VMEM((4, 4, LANES), F32),
        pltpu.VMEM((18, 24, LANES), F32),
        pltpu.VMEM((12, 16, LANES), F32),
        pltpu.VMEM((8, LANES), F32),
        pltpu.VMEM((8, LANES), F32),
        pltpu.VMEM((gy_size, LANES), F32),
        pltpu.VMEM((gy_size, LANES), F32),
        pltpu.VMEM((gx_size, gy_size, LANES), F32),
        pltpu.VMEM((gy_size, LANES), F32),
        pltpu.VMEM((TALLY_ROWS, LANES), F32),
        pltpu.SemaphoreType.DMA((3,)),
        pltpu.SemaphoreType.DMA((11,)),
        pltpu.SemaphoreType.DMA((11,)),
    ]

    def body(*refs):
        kernel(gx_size, gy_size, *refs)

    return pl.pallas_call(
        body,
        out_shape=jax.ShapeDtypeStruct(head.shape, F32),
        in_specs=[pl.BlockSpec(memory_space=pl.ANY)] * 3,
        out_specs=pl.BlockSpec(memory_space=pltpu.VMEM),
        scratch_shapes=scratch,
        compiler_params=pltpu.CompilerParams(
            collective_id=0, has_side_effects=True, vmem_limit_bytes=62 * 1024 * 1024
        ),
        name="vcycle",
    )(head, recharge, conductivity)


def solution(mesh):
    gx_size, gy_size = mesh.shape["gx"], mesh.shape["gy"]

    def one_device(head, recharge, conductivity):
        return on_device(gx_size, gy_size, head, recharge, conductivity)

    spec = P("gx", "gy", None)
    return jax.shard_map(
        one_device, mesh=mesh, in_specs=(spec, spec, spec), out_specs=spec, check_vma=False
    )
```

time: 63 us -> 46.7 us (0.74)
  Pallas kernels: 59.3 us -> 44.9 us
  local copies, waits for them, and re-layouts: 3.55 us -> 1.67 us
    pallas_call x1, Pallas kernels: 59.3 us -> 44.9 us  [on_device(): pl.pallas_call(body, out_shape=jax.ShapeDtypeStruct(head.shape, F32), in_...]
    unnamed x7 -> x1, local copies, waits for them, and re-layouts: 3.55 us -> 1.67 us
where the time goes in v2:
time: 46.7 us; the launch traced here: 46.6 us
  Pallas kernels  44.9 us (96%)
  local copies, waits for them, and re-layouts  1.67 us (4%)
    pallas_call x1, Pallas kernels, on_device(): pl.pallas_call(body, out_shape=jax.ShapeDtypeStruct(head.shape, F32), in_...  44.9 us
    unnamed x1, local copies, waits for them, and re-layouts  1.67 us

profile of v2, /device:TPU:1, one launch (start us, length us, event | category | flops | bytes accessed | tf_op | source)
XLA Modules:
  0.0 46.6 jit_solution(3274309875895353866)
XLA Ops:
  0.0 44.9 %vcycle.1 = f32[32,16,128]{2,1,0:T(8,128)} custom-call(f32[32,16,128]{2,1,0:T(8,128)} %refs_0_.1, f32[32,16,128]{2,1,0:T(8,128)} %refs_1_.1, f32[32,16,128]{2,1,0:T(8,128)} %refs_2_.1), custom_call_target="tpu_custom_call" | custom-call | tf_op jit(solution)/shard_map/vcycle/pallas_call | solution.py:621
  44.9 1.7 %copy.5 = f32[32,16,128]{2,1,0:T(8,128)} copy(f32[32,16,128]{2,1,0:T(8,128)} %vcycle.1) | data formatting | bytes 524288

commit v3 on v2

--- a/solution.py
+++ b/solution.py
@@ -65,8 +65,8 @@
 def swap(value, bit):
     if 2 * bit == LANES:
         return down(value, bit)
-    lane = iota(value.shape, value.ndim - 1)
-    return jnp.where((lane & bit) == 0, up(value, bit), down(value, bit))
+    flat = value.reshape(-1, LANES)
+    return lane_gather(flat, iota(flat.shape, 1) ^ bit).reshape(value.shape)
 
 
 def lane_gather(value, index):
@@ -80,10 +80,13 @@
 
 
 def partners(level, halo):
+    found = []
     for dx in (-1, 0, 1):
         for dy in range(-level.reach, level.reach + 1):
             if (dx, dy) != (0, 0):
-                yield dx, dy, segment(dx, level.bx, halo), segment(dy, level.by, halo)
+                near = halo - 1 if dx and dy and level.span == 1 else halo
+                found.append((dx, dy, segment(dx, level.bx, near), segment(dy, level.by, near)))
+    return sorted(found, key=lambda p: -abs(p[0]) - abs(p[1]))
 
 
 def exchange_rows(level, halo):
@@ -325,11 +328,11 @@
 def solve_5(weight, faces, g):
     start = weight * g
 
-    def step(_, v):
+    v = start
+    for _ in range(COARSE_SWEEPS - 1):
         parts = [c * beyond for c, beyond in zip(faces, sides_5(v))]
-        return (KEEP * v + start) + ((parts[0] + parts[1]) + (parts[2] + parts[3]) + (parts[4] + parts[5]))
-
-    return lax.fori_loop(0, COARSE_SWEEPS - 1, step, start)
+        v = (KEEP * v + start) + ((parts[0] + parts[1]) + (parts[2] + parts[3]) + (parts[4] + parts[5]))
+    return v
 
 
 N_SPLIT = 10
@@ -381,6 +384,17 @@
             barrier, inc=1, device_id=device(dx, dy), device_id_type=pl.DeviceIdType.MESH
         )
 
+    greeted = 0
+    for dx, dy, _, _ in partners(SPLIT[2], 6):
+        greet(dx, dy)
+        greeted += 1
+    for k in range(3, gy_size - 2):
+        greet(0, k)
+        greeted += 1
+    for k in range(2, gx_size - 1):
+        greet(k, 0)
+        greeted += 1
+
     local = [
         pltpu.make_async_copy(
             conductivity,
@@ -397,26 +411,6 @@
     for copy in local:
         copy.start()
 
-    greeted = 0
-    for dx, dy, _, _ in partners(SPLIT[2], 6):
-        greet(dx, dy)
-        greeted += 1
-
-    def greet_y(k, carry):
-        greet(0, k)
-        return carry
-
-    def greet_x(k, carry):
-        greet(k, 0)
-        return carry
-
-    if gy_size > 5:
-        lax.fori_loop(3, gy_size - 2, greet_y, 0)
-        greeted += gy_size - 5
-    if gx_size > 3:
-        lax.fori_loop(2, gx_size - 1, greet_x, 0)
-        greeted += gx_size - 3
-
     for ref in whole:
         ref.clear_edges()
     pl.semaphore_wait(barrier, greeted)
@@ -449,19 +443,16 @@
         block = tally.at[pl.ds(0, rows), :]
         pltpu.make_async_copy(block, block, send_sem.at[stage]).wait()
 
+    def far_first(count):
+        return sorted(range(1, count), key=lambda k: -min(k, count - k))
+
     def gather_y(strip, stage):
-        def step(k, carry):
+        for k in far_first(gy_size):
             push(strip.at[pl.ds(gy, 1), :], strip.at[pl.ds(gy, 1), :], stage, 0, k)
-            return carry
-
-        lax.fori_loop(1, gy_size, step, 0)
 
     def gather_x(strip, place, stage):
-        def step(k, carry):
+        for k in far_first(gx_size):
             push(strip, place, stage, k, 0)
-            return carry
-
-        lax.fori_loop(1, gx_size, step, 0)
 
     lv0, lv1, lv2 = SPLIT
     exchange(lv0, lv0.hk, 0, conductivity, 0, 0, zero.k, 4, PAD + 4)
@@ -513,6 +504,8 @@
     exchange(lv2, lv2.hg, 6, two.g, 5, 6, two.g, 5, 6)
     arrived(5, exchange_rows(lv2, lv2.hk))
     two.faces()
+    arrived(8, (gx_size - 1) * gy_size)
+    three.faces()
     arrived(6, exchange_rows(lv2, lv2.hg))
     two.first_sweep(two.va)
     two.sweep(two.va, two.vb, 4)
@@ -520,16 +513,14 @@
     strip_g[pl.ds(gy, 1), :] = pack_3(rows_g)
 
     gather_y(strip_g, 9)
-    arrived(8, (gx_size - 1) * gy_size)
-    three.faces()
     k4 = 0.125 * octet_3(three.inside(three.k)[...])
     four.inside(four.k)[...] = k4
     rest[...] = k4
     weight5, faces5 = faces_5(pack_5(rest, 1.0, 0.125, gx_size, gy_size), gx_size)
-    four.faces()
     arrived(9, gy_size - 1)
     three.g[pl.ds(gx, 1)] = strip_g[...].reshape(1, gy_size, LANES)
     gather_x(strip_g, three.g.at[gx], 10)
+    four.faces()
     arrived(10, (gx_size - 1) * gy_size)
 
     three.first_sweep(three.va)

time: 46.7 us -> 46.1 us (0.987)
  Pallas kernels: 44.9 us -> 44.3 us
    pallas_call x1, Pallas kernels: 44.9 us -> 44.3 us  [on_device(): pl.pallas_call(body, out_shape=jax.ShapeDtypeStruct(head.shape, F32), in_...]
where the time goes in v3:
time: 46.1 us; the launch traced here: 46 us
  Pallas kernels  44.3 us (96%)
  local copies, waits for them, and re-layouts  1.67 us (4%)
    pallas_call x1, Pallas kernels, on_device(): pl.pallas_call(body, out_shape=jax.ShapeDtypeStruct(head.shape, F32), in_...  44.3 us
    unnamed x1, local copies, waits for them, and re-layouts  1.67 us

profile of v3, /device:TPU:1, one launch (start us, length us, event | category | flops | bytes accessed | tf_op | source)
XLA Modules:
  0.0 46.0 jit_solution(2777350817949396072)
XLA Ops:
  0.0 44.3 %vcycle.1 = f32[32,16,128]{2,1,0:T(8,128)} custom-call(f32[32,16,128]{2,1,0:T(8,128)} %refs_0_.1, f32[32,16,128]{2,1,0:T(8,128)} %refs_1_.1, f32[32,16,128]{2,1,0:T(8,128)} %refs_2_.1), custom_call_target="tpu_custom_call" | custom-call | tf_op jit(solution)/shard_map/vcycle/pallas_call | solution.py:612
  44.3 1.7 %copy.5 = f32[32,16,128]{2,1,0:T(8,128)} copy(f32[32,16,128]{2,1,0:T(8,128)} %vcycle.1) | data formatting | bytes 524288

commit v4 on v3

--- a/solution.py
+++ b/solution.py
@@ -32,7 +32,7 @@
 
 SPLIT = (
     Level(32, 16, 3, 24, 4, 1, 1, 4, 3, 24),
-    Level(16, 8, 4, 16, 4, 2, 1, 5, 4, 24),
+    Level(16, 8, 6, 24, 8, 2, 1, 7, 6, 24),
     Level(8, 4, 5, 16, 6, 4, 2, 6, 5, 16),
 )
 
@@ -84,7 +84,7 @@
     for dx in (-1, 0, 1):
         for dy in range(-level.reach, level.reach + 1):
             if (dx, dy) != (0, 0):
-                near = halo - 1 if dx and dy and level.span == 1 else halo
+                near = halo - 1 if dx and dy and level.span <= 2 else halo
                 found.append((dx, dy, segment(dx, level.bx, near), segment(dy, level.by, near)))
     return sorted(found, key=lambda p: -abs(p[0]) - abs(p[1]))
 
@@ -163,15 +163,17 @@
         along_z = self.czl[x, own, :] * down(here, span) + self.czh[x, own, :] * up(here, span)
         return here, (along_x + along_y) + along_z
 
-    def first_sweep(self, dst):
-        dst[pl.ds(1, self.at.bx + 2 * self.at.hx), pl.ds(PAD, self.at.rows), :] = self.w[...] * self.g[...]
-
-    def sweep(self, src, dst, halo):
+    def first_sweep(self, dst, halo, g):
+        low, count = self.at.hx - halo, self.at.bx + 2 * halo
+        x = pl.ds(low, count)
+        dst[pl.ds(low + 1, count), pl.ds(PAD, self.at.rows), :] = self.w[x] * g[x]
+
+    def sweep(self, src, dst, halo, g):
         lv = self.at
         low, count = lv.hx - halo, lv.bx + 2 * halo
         here, total = self.beside(src, low, count, 0, lv.rows)
         x = pl.ds(low, count)
-        dst[pl.ds(low + 1, count), pl.ds(PAD, lv.rows), :] = KEEP * here + self.w[x] * (self.g[x] + total)
+        dst[pl.ds(low + 1, count), pl.ds(PAD, lv.rows), :] = KEEP * here + self.w[x] * (g[x] + total)
 
     def last_sweep(self, src, out):
         lv = self.at
@@ -179,10 +181,12 @@
         here, total = self.beside(src, lv.hx, lv.bx, lv.first, lv.by)
         out[...] = KEEP * here + self.w[x, own, :] * (self.g[x, own, :] + total)
 
-    def residual(self, v):
+    def residual(self, v, halo):
         lv = self.at
-        x, own = pl.ds(lv.hx, lv.bx), pl.ds(lv.first, lv.by)
-        here, total = self.beside(v, lv.hx, lv.bx, lv.first, lv.by)
+        low, count = lv.hx - halo, lv.bx + 2 * halo
+        row, rows = lv.first - halo, lv.by + 2 * halo
+        x, own = pl.ds(low, count), pl.ds(row, rows)
+        here, total = self.beside(v, low, count, row, rows)
         return self.g[x, own, :] + total - self.d[x, own, :] * here
 
     def correct(self, v, coarse, x0, count, wide):
@@ -354,7 +358,9 @@
     (
         half0,
         half1,
+        half1_k,
         half2,
+        wide_g,
         wide0,
         wide1,
         rows_k,
@@ -470,12 +476,12 @@
 
     local[0].wait()
     own0 = (pl.ds(4, BLOCK_X), pl.ds(PAD + 4, BLOCK_Y))
-    own1, own2 = (pl.ds(5, 16), pl.ds(PAD + 4, 8)), (pl.ds(6, 8), pl.ds(PAD + 6, 4))
+    own1, own2 = (pl.ds(7, 16), pl.ds(PAD + 8, 8)), (pl.ds(6, 8), pl.ds(PAD + 6, 4))
     one.k[own1] = restrict(zero.k[own0], half0, 1, 0.125)
-    two.k[own2] = restrict(one.k[own1], half1, 2, 0.125)
+    two.k[own2] = restrict(one.k[own1], half1_k, 2, 0.125)
     to_rows(restrict(two.k[own2], half2, 4, 0.125), rows_k)
     strip_k[pl.ds(gy, 1), :] = pack_3(rows_k)
-    exchange(lv1, lv1.hk, 3, one.k, 5, PAD + 4, one.k, 5, PAD + 4)
+    exchange(lv1, lv1.hk, 3, one.k, 7, PAD + 8, one.k, 7, PAD + 8)
     gather_y(strip_k, 7)
     exchange(lv2, lv2.hk, 5, two.k, 6, PAD + 6, two.k, 6, PAD + 6)
 
@@ -489,30 +495,30 @@
     local[2].wait()
     arrived(1, exchange_rows(lv0, 4))
     arrived(2, exchange_rows(lv0, lv0.hg))
-    zero.sweep(zero.va, zero.vb, 3)
-    zero.sweep(zero.vb, zero.va, 2)
-    one.g[pl.ds(4, 16), pl.ds(4, 8), :] = restrict(zero.residual(zero.va), half0, 1, 0.5)
-
-    exchange(lv1, lv1.hg, 4, one.g, 4, 4, one.g, 4, 4)
+    zero.sweep(zero.va, zero.vb, 3, zero.g)
+    zero.sweep(zero.vb, zero.va, 2, zero.g)
+    one.g[pl.ds(6, 16), pl.ds(8, 8), :] = restrict(zero.residual(zero.va, 0), half0, 1, 0.5)
+
+    exchange(lv1, lv1.hg, 4, one.g, 6, 8, one.g, 6, 8)
     arrived(3, exchange_rows(lv1, lv1.hk))
     one.faces()
-    arrived(4, exchange_rows(lv1, lv1.hg))
-    one.first_sweep(one.va)
-    one.sweep(one.va, one.vb, 3)
-    two.g[pl.ds(5, 8), pl.ds(6, 4), :] = restrict(one.residual(one.vb), half1, 2, 0.5)
-
-    exchange(lv2, lv2.hg, 6, two.g, 5, 6, two.g, 5, 6)
     arrived(5, exchange_rows(lv2, lv2.hk))
     two.faces()
     arrived(8, (gx_size - 1) * gy_size)
     three.faces()
-    arrived(6, exchange_rows(lv2, lv2.hg))
-    two.first_sweep(two.va)
-    two.sweep(two.va, two.vb, 4)
-    to_rows(restrict(two.residual(two.vb), half2, 4, 0.5), rows_g)
+    arrived(4, exchange_rows(lv1, lv1.hg))
+    one.first_sweep(one.va, 6, one.g)
+    one.sweep(one.va, one.vb, 5, one.g)
+    two.g[pl.ds(3, 12), pl.ds(4, 8), :] = restrict(one.residual(one.vb, 4), half1, 2, 0.5)
+    two.first_sweep(two.va, 2, two.g)
+    two.sweep(two.va, two.vb, 1, two.g)
+    to_rows(restrict(two.residual(two.vb, 0), half2, 4, 0.5), rows_g)
     strip_g[pl.ds(gy, 1), :] = pack_3(rows_g)
 
     gather_y(strip_g, 9)
+    own_g = (pl.ds(5, 8), pl.ds(6, 4))
+    wide_g[own_g] = two.g[own_g]
+    exchange(lv2, lv2.hg, 6, wide_g, 5, 6, wide_g, 5, 6)
     k4 = 0.125 * octet_3(three.inside(three.k)[...])
     four.inside(four.k)[...] = k4
     rest[...] = k4
@@ -520,6 +526,9 @@
     arrived(9, gy_size - 1)
     three.g[pl.ds(gx, 1)] = strip_g[...].reshape(1, gy_size, LANES)
     gather_x(strip_g, three.g.at[gx], 10)
+    arrived(6, exchange_rows(lv2, lv2.hg))
+    two.first_sweep(two.va, 5, wide_g)
+    two.sweep(two.va, two.vb, 4, wide_g)
     four.faces()
     arrived(10, (gx_size - 1) * gy_size)
 
@@ -559,14 +568,14 @@
             for child in range(2):
                 place = (2 * (4 * dx + x) + child + 6, pl.ds(PAD, lv2.rows))
                 two.vb[place] = two.vb[place] + copies
-    two.sweep(two.vb, two.va, 3)
-    two.sweep(two.va, two.vb, 2)
-
-    one.correct(one.vb, two.vb[pl.ds(4, 12), pl.ds(PAD + 4, 8), :], 1, 12, wide1)
-    one.sweep(one.vb, one.va, 2)
-    one.sweep(one.va, one.vb, 1)
-    zero.correct(zero.va, one.vb[pl.ds(4, 18), pl.ds(PAD + 2, 12), :], 2, 18, wide0)
-    zero.sweep(zero.va, zero.vb, 1)
+    two.sweep(two.vb, two.va, 3, wide_g)
+    two.sweep(two.va, two.vb, 2, wide_g)
+
+    one.correct(one.vb, two.vb[pl.ds(4, 12), pl.ds(PAD + 2, 12), :], 3, 12, wide1)
+    one.sweep(one.vb, one.va, 2, one.g)
+    one.sweep(one.va, one.vb, 1, one.g)
+    zero.correct(zero.va, one.vb[pl.ds(6, 18), pl.ds(PAD + 6, 12), :], 2, 18, wide0)
+    zero.sweep(zero.va, zero.vb, 1, zero.g)
     zero.last_sweep(zero.vb, out)
 
     sent(0, exchange_rows(lv0, lv0.hk))
@@ -590,10 +599,12 @@
         scratch += Whole.scratch(gx_size, gy_size)
     scratch += [
         pltpu.VMEM((16, 16, LANES), F32),
+        pltpu.VMEM((12, 16, LANES), F32),
         pltpu.VMEM((8, 8, LANES), F32),
         pltpu.VMEM((4, 4, LANES), F32),
+        pltpu.VMEM((18, 16, LANES), F32),
         pltpu.VMEM((18, 24, LANES), F32),
-        pltpu.VMEM((12, 16, LANES), F32),
+        pltpu.VMEM((12, 24, LANES), F32),
         pltpu.VMEM((8, LANES), F32),
         pltpu.VMEM((8, LANES), F32),
         pltpu.VMEM((gy_size, LANES), F32),

time: 46.1 us -> 42.4 us (0.920)
  Pallas kernels: 44.3 us -> 40.6 us
    pallas_call x1, Pallas kernels: 44.3 us -> 40.6 us  [on_device(): pl.pallas_call(body, out_shape=jax.ShapeDtypeStruct(head.shape, F32), in_...]
where the time goes in v4:
time: 42.4 us; the launch traced here: 42.3 us
  Pallas kernels  40.6 us (96%)
  local copies, waits for them, and re-layouts  1.67 us (4%)
    pallas_call x1, Pallas kernels, on_device(): pl.pallas_call(body, out_shape=jax.ShapeDtypeStruct(head.shape, F32), in_...  40.6 us
    unnamed x1, local copies, waits for them, and re-layouts  1.67 us

profile of v4, /device:TPU:1, one launch (start us, length us, event | category | flops | bytes accessed | tf_op | source)
XLA Modules:
  0.0 42.3 jit_solution(7984876695498059061)
XLA Ops:
  0.0 40.6 %vcycle.1 = f32[32,16,128]{2,1,0:T(8,128)} custom-call(f32[32,16,128]{2,1,0:T(8,128)} %refs_0_.1, f32[32,16,128]{2,1,0:T(8,128)} %refs_1_.1, f32[32,16,128]{2,1,0:T(8,128)} %refs_2_.1), custom_call_target="tpu_custom_call" | custom-call | tf_op jit(solution)/shard_map/vcycle/pallas_call | solution.py:623
  40.6 1.7 %copy.5 = f32[32,16,128]{2,1,0:T(8,128)} copy(f32[32,16,128]{2,1,0:T(8,128)} %vcycle.1) | data formatting | bytes 524288

commit v5 on v4

--- a/solution.py
+++ b/solution.py
@@ -10,6 +10,7 @@
 F32 = jnp.float32
 LANES = 128
 PAD = 8
+EDGE = 6
 OMEGA = 0.8
 KEEP = 1.0 - OMEGA
 COARSE_SWEEPS = 16
@@ -211,30 +212,37 @@
     def __init__(self, number, nx, ny, refs):
         self.number, self.nx, self.ny = number, nx, ny
         self.k, self.va, self.vb, self.g, self.c, self.w, self.d = refs
+        self.all = (EDGE, nx)
 
     @staticmethod
     def scratch(nx, ny):
-        padded = pltpu.VMEM((nx + 2, ny + 2 * PAD, LANES), F32)
-        plain = pltpu.VMEM((nx, ny, LANES), F32)
-        return [padded, padded, padded, plain, pltpu.VMEM((6, nx, ny, LANES), F32), plain, plain]
+        x = nx + 2 * EDGE
+        padded = pltpu.VMEM((x, ny + 2 * PAD, LANES), F32)
+        plain = pltpu.VMEM((x, ny, LANES), F32)
+        return [padded, padded, padded, plain, pltpu.VMEM((6, x, ny, LANES), F32), plain, plain]
 
     def clear_edges(self):
+        for x in (0, EDGE + self.nx):
+            layers = pl.ds(x, EDGE)
+            for ref in (self.k, self.va, self.vb, self.g, self.w):
+                ref[layers] = jnp.zeros((EDGE,) + ref.shape[1:], F32)
+            self.c[:, layers] = jnp.zeros((6, EDGE, self.ny, LANES), F32)
         for ref in (self.k, self.va, self.vb):
-            for x in (0, self.nx + 1):
-                ref[x] = jnp.zeros((self.ny + 2 * PAD, LANES), F32)
             for row in (0, PAD + self.ny):
-                ref[:, pl.ds(row, PAD), :] = jnp.zeros((self.nx + 2, PAD, LANES), F32)
-
-    def inside(self, ref):
-        return ref.at[pl.ds(1, self.nx), pl.ds(PAD, self.ny), :]
-
-    def neighbours(self, v):
-        inner, all_x = pl.ds(PAD, self.ny), pl.ds(1, self.nx)
-        here = v[all_x, inner, :]
-        before = v[pl.ds(0, self.nx), inner, :]
-        after = v[pl.ds(2, self.nx), inner, :]
-        under = v[all_x, pl.ds(PAD - 1, self.ny), :]
-        over = v[all_x, pl.ds(PAD + 1, self.ny), :]
+                ref[pl.ds(EDGE, self.nx), pl.ds(row, PAD), :] = jnp.zeros((self.nx, PAD, LANES), F32)
+
+    def inside(self, ref, layers=None):
+        start, count = layers or self.all
+        return ref.at[pl.ds(start, count), pl.ds(PAD, self.ny), :]
+
+    def neighbours(self, v, layers):
+        start, count = layers
+        inner, mid = pl.ds(PAD, self.ny), pl.ds(start, count)
+        here = v[mid, inner, :]
+        before = v[pl.ds(start - 1, count), inner, :]
+        after = v[pl.ds(start + 1, count), inner, :]
+        under = v[mid, pl.ds(PAD - 1, self.ny), :]
+        over = v[mid, pl.ds(PAD + 1, self.ny), :]
         lane = iota((1, self.ny, LANES), 2)
         if self.number == 3:
             before = down(jnp.where(lane >= 96, before, here), 32)
@@ -261,33 +269,38 @@
             first_x, last_x, first_y, last_y = lane < 64, lane >= 64, row == 0, row == self.ny - 1
             first_z, last_z = z < 2, z >= 14
         first_x, last_x = (x == 0) & first_x, (x == self.nx - 1) & last_x
-        sides, here = self.neighbours(self.k)
+        sides, here = self.neighbours(self.k, self.all)
+        inside = pl.ds(*self.all)
         total = jnp.zeros(shape, F32)
         for n, cut in enumerate((first_x, last_x, first_y, last_y, first_z, last_z)):
             value = face(here, sides[n])
-            self.c[n] = jnp.where(cut, 0.0, value)
+            self.c[n, inside] = jnp.where(cut, 0.0, value)
             total = total + jnp.where(cut, here, value)
-        self.d[...] = total
-        self.w[...] = OMEGA * reciprocal(total)
-
-    def beside(self, v):
-        sides, here = self.neighbours(v)
-        parts = [self.c[n] * sides[n] for n in range(6)]
+        self.d[inside] = total
+        self.w[inside] = OMEGA * reciprocal(total)
+
+    def beside(self, v, layers):
+        sides, here = self.neighbours(v, layers)
+        parts = [self.c[n, pl.ds(*layers)] * sides[n] for n in range(6)]
         return here, (parts[0] + parts[1]) + (parts[2] + parts[3]) + (parts[4] + parts[5])
 
     def first_sweep(self, dst):
-        self.inside(dst)[...] = self.w[...] * self.g[...]
-
-    def sweep(self, src, dst):
-        here, total = self.beside(src)
-        self.inside(dst)[...] = KEEP * here + self.w[...] * (self.g[...] + total)
+        x = pl.ds(*self.all)
+        self.inside(dst)[...] = self.w[x] * self.g[x]
+
+    def sweep(self, src, dst, layers=None):
+        layers = layers or self.all
+        x = pl.ds(*layers)
+        here, total = self.beside(src, layers)
+        self.inside(dst, layers)[...] = KEEP * here + self.w[x] * (self.g[x] + total)
 
     def residual(self, v):
-        here, total = self.beside(v)
-        return self.g[...] + total - self.d[...] * here
-
-    def correct(self, v, values):
-        place = self.inside(v)
+        x = pl.ds(*self.all)
+        here, total = self.beside(v, self.all)
+        return self.g[x] + total - self.d[x] * here
+
+    def correct(self, v, layers, values):
+        place = self.inside(v, layers)
         place[...] = place[...] + values
 
 
@@ -301,10 +314,10 @@
     half = ny // 2
     shape = (nx, half, LANES)
     rows = ref[:, pl.ds(0, half, stride=2), :] + ref[:, pl.ds(1, half, stride=2), :]
-    rows = rows + swap(rows, 2)
-    rows = scale * (rows + swap(rows, 64))
+    rows = scale * rows.reshape(nx * half, LANES)
     index = (iota((nx * half, LANES), 1) & 3) * 4
-    rows = lane_gather(rows.reshape(nx * half, LANES), index).reshape(shape)
+    children = [lane_gather(rows, index + child) for child in (0, 2, 64, 66)]
+    rows = ((children[0] + children[1]) + (children[2] + children[3])).reshape(shape)
     packed = jnp.sum(jnp.where((iota(shape, 2) >> 2) == iota(shape, 0), rows, 0.0), axis=0)
     return packed + jnp.where(iota((half, LANES), 1) >= 4 * nx, fill, 0.0)
 
@@ -417,8 +430,6 @@
     for copy in local:
         copy.start()
 
-    for ref in whole:
-        ref.clear_edges()
     pl.semaphore_wait(barrier, greeted)
 
     def push(src, dst, stage, dx, dy):
@@ -431,15 +442,16 @@
             device_id_type=pl.DeviceIdType.MESH,
         ).start()
 
-    def exchange(level, halo, stage, src, src_x, src_row, dst, dst_x, dst_row):
+    def exchange(level, halo, stage, src, src_x, src_row, dst, dst_x, dst_row, far=(True, False)):
         for dx, dy, xs, ys in partners(level, halo):
-            push(
-                src.at[pl.ds(src_x + xs[0], xs[1]), pl.ds(src_row + ys[0], ys[1]), :],
-                dst.at[pl.ds(dst_x + xs[2], xs[1]), pl.ds(dst_row + ys[2], ys[1]), :],
-                stage,
-                dx,
-                dy,
-            )
+            if (dx != 0 and dy != 0) in far:
+                push(
+                    src.at[pl.ds(src_x + xs[0], xs[1]), pl.ds(src_row + ys[0], ys[1]), :],
+                    dst.at[pl.ds(dst_x + xs[2], xs[1]), pl.ds(dst_row + ys[2], ys[1]), :],
+                    stage,
+                    dx,
+                    dy,
+                )
 
     def arrived(stage, rows):
         block = tally.at[pl.ds(0, rows), :]
@@ -461,9 +473,10 @@
             push(strip, place, stage, k, 0)
 
     lv0, lv1, lv2 = SPLIT
-    exchange(lv0, lv0.hk, 0, conductivity, 0, 0, zero.k, 4, PAD + 4)
-    exchange(lv0, 4, 1, head, 0, 0, zero.va, 4, PAD + 4)
-    exchange(lv0, lv0.hg, 2, recharge, 0, 0, zero.g, 3, 4)
+    for far in ((True,), (False,)):
+        exchange(lv0, lv0.hk, 0, conductivity, 0, 0, zero.k, 4, PAD + 4, far)
+        exchange(lv0, 4, 1, head, 0, 0, zero.va, 4, PAD + 4, far)
+        exchange(lv0, lv0.hg, 2, recharge, 0, 0, zero.g, 3, 4, far)
 
     def pack_3(rows):
         lane, row = iota((8, LANES), 1), iota((8, LANES), 0)
@@ -485,12 +498,15 @@
     gather_y(strip_k, 7)
     exchange(lv2, lv2.hk, 5, two.k, 6, PAD + 6, two.k, 6, PAD + 6)
 
+    for ref in whole:
+        ref.clear_edges()
+
     arrived(0, exchange_rows(lv0, lv0.hk))
     zero.faces()
     arrived(7, gy_size - 1)
     inner = pl.ds(PAD, gy_size)
-    three.k[pl.ds(gx + 1, 1), inner, :] = strip_k[...].reshape(1, gy_size, LANES)
-    gather_x(strip_k, three.k.at[gx + 1, inner, :], 8)
+    three.k[pl.ds(gx + EDGE, 1), inner, :] = strip_k[...].reshape(1, gy_size, LANES)
+    gather_x(strip_k, three.k.at[gx + EDGE, inner, :], 8)
     local[1].wait()
     local[2].wait()
     arrived(1, exchange_rows(lv0, 4))
@@ -524,17 +540,25 @@
     rest[...] = k4
     weight5, faces5 = faces_5(pack_5(rest, 1.0, 0.125, gx_size, gy_size), gx_size)
     arrived(9, gy_size - 1)
-    three.g[pl.ds(gx, 1)] = strip_g[...].reshape(1, gy_size, LANES)
-    gather_x(strip_g, three.g.at[gx], 10)
+    three.g[pl.ds(gx + EDGE, 1)] = strip_g[...].reshape(1, gy_size, LANES)
+    gather_x(strip_g, three.g.at[gx + EDGE], 10)
     arrived(6, exchange_rows(lv2, lv2.hg))
     two.first_sweep(two.va, 5, wide_g)
     two.sweep(two.va, two.vb, 4, wide_g)
     four.faces()
+    sent(0, exchange_rows(lv0, lv0.hk))
+    sent(1, exchange_rows(lv0, 4))
+    sent(2, exchange_rows(lv0, lv0.hg))
+    sent(3, exchange_rows(lv1, lv1.hk))
+    sent(4, exchange_rows(lv1, lv1.hg))
+    sent(5, exchange_rows(lv2, lv2.hk))
+    sent(7, gy_size - 1)
+    sent(8, (gx_size - 1) * gy_size)
     arrived(10, (gx_size - 1) * gy_size)
 
     three.first_sweep(three.va)
     three.sweep(three.va, three.vb)
-    four.g[...] = 0.5 * octet_3(three.residual(three.vb))
+    four.g[pl.ds(*four.all)] = 0.5 * octet_3(three.residual(three.vb))
     four.first_sweep(four.va)
     four.sweep(four.va, four.vb)
     rest[...] = four.residual(four.vb)
@@ -542,26 +566,28 @@
 
     coarse5[pl.ds(0, gy_size // 2, stride=2), :] = v5
     coarse5[pl.ds(1, gy_size // 2, stride=2), :] = v5
-    shape = (gx_size, gy_size, LANES)
-    flat = (gx_size * gy_size, LANES)
-    index = iota(shape, 0) * 4 + ((iota(shape, 2) & 15) >> 2)
+    def layers(reach):
+        return gx + (EDGE - reach), 2 * reach + 1
+
+    shape = (11, gy_size, LANES)
+    flat = (11 * gy_size, LANES)
+    index = ((gx - 5 + iota(shape, 0)) * 4 + ((iota(shape, 2) & 15) >> 2)) & (LANES - 1)
     wide5 = jnp.broadcast_to(coarse5[...][None], shape).reshape(flat)
-    four.correct(four.vb, lane_gather(wide5, index.reshape(flat)).reshape(shape))
-    four.sweep(four.vb, four.va)
-    four.sweep(four.va, four.vb)
-    three.correct(three.vb, four.inside(four.vb)[...])
-    three.sweep(three.vb, three.va)
-    three.sweep(three.va, three.vb)
+    four.correct(four.vb, layers(5), lane_gather(wide5, index.reshape(flat)).reshape(shape))
+    four.sweep(four.vb, four.va, layers(4))
+    four.sweep(four.va, four.vb, layers(3))
+    three.correct(three.vb, layers(3), four.inside(four.vb, layers(3))[...])
+    three.sweep(three.vb, three.va, layers(2))
+    three.sweep(three.va, three.vb, layers(1))
 
     row = iota((lv2.rows, LANES), 0)
     lane = iota((lv2.rows, LANES), 1)
     y3 = (row >> 1) - 1
     for dx in (-1, 0, 1):
-        gxn = lax.rem(gx + (dx + gx_size), gx_size) + 1
         near = []
         for dy in (-1, 0, 1):
-            gyn = lax.rem(gy + (dy + gy_size), gy_size) + PAD
-            near.append(three.vb[pl.ds(gxn, 1), pl.ds(gyn, 1), :].reshape(1, LANES))
+            place = (pl.ds(gx + (dx + EDGE), 1), pl.ds(gy + (dy + PAD), 1))
+            near.append(three.vb[place].reshape(1, LANES))
         rows = jnp.where(y3 < 2, near[0], jnp.where(y3 < 4, near[1], near[2]))
         for x in ((2, 3), (0, 1, 2, 3), (0, 1))[dx + 1]:
             copies = lane_gather(rows, (2 * x + (y3 & 1)) * 16 + (lane >> 3))
@@ -578,16 +604,8 @@
     zero.sweep(zero.va, zero.vb, 1, zero.g)
     zero.last_sweep(zero.vb, out)
 
-    sent(0, exchange_rows(lv0, lv0.hk))
-    sent(1, exchange_rows(lv0, 4))
-    sent(2, exchange_rows(lv0, lv0.hg))
-    sent(3, exchange_rows(lv1, lv1.hk))
-    sent(4, exchange_rows(lv1, lv1.hg))
-    sent(5, exchange_rows(lv2, lv2.hk))
+    sent(9, gy_size - 1)
     sent(6, exchange_rows(lv2, lv2.hg))
-    sent(7, gy_size - 1)
-    sent(8, (gx_size - 1) * gy_size)
-    sent(9, gy_size - 1)
     sent(10, (gx_size - 1) * gy_size)
 
 

time: 42.4 us -> 41.9 us (0.988)
  Pallas kernels: 40.6 us -> 40.1 us
    pallas_call x1, Pallas kernels: 40.6 us -> 40.1 us  [on_device(): pl.pallas_call(body, out_shape=jax.ShapeDtypeStruct(head.shape, F32), in_...]
where the time goes in v5:
time: 41.9 us; the launch traced here: 41.8 us
  Pallas kernels  40.1 us (96%)
  local copies, waits for them, and re-layouts  1.67 us (4%)
    pallas_call x1, Pallas kernels, on_device(): pl.pallas_call(body, out_shape=jax.ShapeDtypeStruct(head.shape, F32), in_...  40.1 us
    unnamed x1, local copies, waits for them, and re-layouts  1.67 us

profile of v5, /device:TPU:1, one launch (start us, length us, event | category | flops | bytes accessed | tf_op | source)
XLA Modules:
  0.0 41.8 jit_solution(3588864117574850032)
XLA Ops:
  0.0 40.1 %vcycle.1 = f32[32,16,128]{2,1,0:T(8,128)} custom-call(f32[32,16,128]{2,1,0:T(8,128)} %refs_0_.1, f32[32,16,128]{2,1,0:T(8,128)} %refs_1_.1, f32[32,16,128]{2,1,0:T(8,128)} %refs_2_.1), custom_call_target="tpu_custom_call" | custom-call | tf_op jit(solution)/shard_map/vcycle/pallas_call | solution.py:641
  40.1 1.7 %copy.5 = f32[32,16,128]{2,1,0:T(8,128)} copy(f32[32,16,128]{2,1,0:T(8,128)} %vcycle.1) | data formatting | bytes 524288

commit v6 on v5

--- a/solution.py
+++ b/solution.py
@@ -495,18 +495,14 @@
     to_rows(restrict(two.k[own2], half2, 4, 0.125), rows_k)
     strip_k[pl.ds(gy, 1), :] = pack_3(rows_k)
     exchange(lv1, lv1.hk, 3, one.k, 7, PAD + 8, one.k, 7, PAD + 8)
+    exchange(lv2, lv2.hk, 5, two.k, 6, PAD + 6, two.k, 6, PAD + 6)
     gather_y(strip_k, 7)
-    exchange(lv2, lv2.hk, 5, two.k, 6, PAD + 6, two.k, 6, PAD + 6)
 
     for ref in whole:
         ref.clear_edges()
 
     arrived(0, exchange_rows(lv0, lv0.hk))
     zero.faces()
-    arrived(7, gy_size - 1)
-    inner = pl.ds(PAD, gy_size)
-    three.k[pl.ds(gx + EDGE, 1), inner, :] = strip_k[...].reshape(1, gy_size, LANES)
-    gather_x(strip_k, three.k.at[gx + EDGE, inner, :], 8)
     local[1].wait()
     local[2].wait()
     arrived(1, exchange_rows(lv0, 4))
@@ -516,12 +512,14 @@
     one.g[pl.ds(6, 16), pl.ds(8, 8), :] = restrict(zero.residual(zero.va, 0), half0, 1, 0.5)
 
     exchange(lv1, lv1.hg, 4, one.g, 6, 8, one.g, 6, 8)
+    arrived(7, gy_size - 1)
+    inner = pl.ds(PAD, gy_size)
+    three.k[pl.ds(gx + EDGE, 1), inner, :] = strip_k[...].reshape(1, gy_size, LANES)
+    gather_x(strip_k, three.k.at[gx + EDGE, inner, :], 8)
     arrived(3, exchange_rows(lv1, lv1.hk))
     one.faces()
     arrived(5, exchange_rows(lv2, lv2.hk))
     two.faces()
-    arrived(8, (gx_size - 1) * gy_size)
-    three.faces()
     arrived(4, exchange_rows(lv1, lv1.hg))
     one.first_sweep(one.va, 6, one.g)
     one.sweep(one.va, one.vb, 5, one.g)
@@ -535,6 +533,8 @@
     own_g = (pl.ds(5, 8), pl.ds(6, 4))
     wide_g[own_g] = two.g[own_g]
     exchange(lv2, lv2.hg, 6, wide_g, 5, 6, wide_g, 5, 6)
+    arrived(8, (gx_size - 1) * gy_size)
+    three.faces()
     k4 = 0.125 * octet_3(three.inside(three.k)[...])
     four.inside(four.k)[...] = k4
     rest[...] = k4

time: 41.9 us -> 40.1 us (0.957)
  Pallas kernels: 40.1 us -> 38.4 us
    pallas_call x1, Pallas kernels: 40.1 us -> 38.4 us  [on_device(): pl.pallas_call(body, out_shape=jax.ShapeDtypeStruct(head.shape, F32), in_...]
where the time goes in v6:
time: 40.1 us; the launch traced here: 40 us
  Pallas kernels  38.4 us (96%)
  local copies, waits for them, and re-layouts  1.67 us (4%)
    pallas_call x1, Pallas kernels, on_device(): pl.pallas_call(body, out_shape=jax.ShapeDtypeStruct(head.shape, F32), in_...  38.4 us
    unnamed x1, local copies, waits for them, and re-layouts  1.67 us

profile of v6, /device:TPU:1, one launch (start us, length us, event | category | flops | bytes accessed | tf_op | source)
XLA Modules:
  0.0 40.0 jit_solution(12444992637124253242)
XLA Ops:
  0.0 38.4 %vcycle.1 = f32[32,16,128]{2,1,0:T(8,128)} custom-call(f32[32,16,128]{2,1,0:T(8,128)} %refs_0_.1, f32[32,16,128]{2,1,0:T(8,128)} %refs_1_.1, f32[32,16,128]{2,1,0:T(8,128)} %refs_2_.1), custom_call_target="tpu_custom_call" | custom-call | tf_op jit(solution)/shard_map/vcycle/pallas_call | solution.py:641
  38.4 1.7 %copy.5 = f32[32,16,128]{2,1,0:T(8,128)} copy(f32[32,16,128]{2,1,0:T(8,128)} %vcycle.1) | data formatting | bytes 524288

commit v7 on v6

--- a/solution.py
+++ b/solution.py
@@ -403,16 +403,11 @@
             barrier, inc=1, device_id=device(dx, dy), device_id_type=pl.DeviceIdType.MESH
         )
 
-    greeted = 0
-    for dx, dy, _, _ in partners(SPLIT[2], 6):
+    guests = [(0, k) for k in range(3, gy_size - 2)] + [(k, 0) for k in range(2, gx_size - 1)]
+    guests.sort(key=lambda g: -min(g[0], gx_size - g[0]) - min(g[1], gy_size - g[1]))
+    guests += [(dx, dy) for dx, dy, _, _ in partners(SPLIT[2], 6)]
+    for dx, dy in guests:
         greet(dx, dy)
-        greeted += 1
-    for k in range(3, gy_size - 2):
-        greet(0, k)
-        greeted += 1
-    for k in range(2, gx_size - 1):
-        greet(k, 0)
-        greeted += 1
 
     local = [
         pltpu.make_async_copy(
@@ -430,7 +425,7 @@
     for copy in local:
         copy.start()
 
-    pl.semaphore_wait(barrier, greeted)
+    pl.semaphore_wait(barrier, len(guests))
 
     def push(src, dst, stage, dx, dy):
         pltpu.make_async_remote_copy(
@@ -496,10 +491,7 @@
     strip_k[pl.ds(gy, 1), :] = pack_3(rows_k)
     exchange(lv1, lv1.hk, 3, one.k, 7, PAD + 8, one.k, 7, PAD + 8)
     exchange(lv2, lv2.hk, 5, two.k, 6, PAD + 6, two.k, 6, PAD + 6)
-    gather_y(strip_k, 7)
-
-    for ref in whole:
-        ref.clear_edges()
+
 
     arrived(0, exchange_rows(lv0, lv0.hk))
     zero.faces()
@@ -512,10 +504,9 @@
     one.g[pl.ds(6, 16), pl.ds(8, 8), :] = restrict(zero.residual(zero.va, 0), half0, 1, 0.5)
 
     exchange(lv1, lv1.hg, 4, one.g, 6, 8, one.g, 6, 8)
-    arrived(7, gy_size - 1)
-    inner = pl.ds(PAD, gy_size)
-    three.k[pl.ds(gx + EDGE, 1), inner, :] = strip_k[...].reshape(1, gy_size, LANES)
-    gather_x(strip_k, three.k.at[gx + EDGE, inner, :], 8)
+    gather_y(strip_k, 7)
+    for ref in whole:
+        ref.clear_edges()
     arrived(3, exchange_rows(lv1, lv1.hk))
     one.faces()
     arrived(5, exchange_rows(lv2, lv2.hk))
@@ -530,22 +521,26 @@
     strip_g[pl.ds(gy, 1), :] = pack_3(rows_g)
 
     gather_y(strip_g, 9)
+    arrived(7, gy_size - 1)
+    inner = pl.ds(PAD, gy_size)
+    three.k[pl.ds(gx + EDGE, 1), inner, :] = strip_k[...].reshape(1, gy_size, LANES)
+    gather_x(strip_k, three.k.at[gx + EDGE, inner, :], 8)
     own_g = (pl.ds(5, 8), pl.ds(6, 4))
     wide_g[own_g] = two.g[own_g]
     exchange(lv2, lv2.hg, 6, wide_g, 5, 6, wide_g, 5, 6)
+    arrived(9, gy_size - 1)
+    three.g[pl.ds(gx + EDGE, 1)] = strip_g[...].reshape(1, gy_size, LANES)
+    gather_x(strip_g, three.g.at[gx + EDGE], 10)
     arrived(8, (gx_size - 1) * gy_size)
     three.faces()
     k4 = 0.125 * octet_3(three.inside(three.k)[...])
     four.inside(four.k)[...] = k4
     rest[...] = k4
     weight5, faces5 = faces_5(pack_5(rest, 1.0, 0.125, gx_size, gy_size), gx_size)
-    arrived(9, gy_size - 1)
-    three.g[pl.ds(gx + EDGE, 1)] = strip_g[...].reshape(1, gy_size, LANES)
-    gather_x(strip_g, three.g.at[gx + EDGE], 10)
+    four.faces()
     arrived(6, exchange_rows(lv2, lv2.hg))
     two.first_sweep(two.va, 5, wide_g)
     two.sweep(two.va, two.vb, 4, wide_g)
-    four.faces()
     sent(0, exchange_rows(lv0, lv0.hk))
     sent(1, exchange_rows(lv0, 4))
     sent(2, exchange_rows(lv0, lv0.hg))

time: 40.1 us -> 39.7 us (0.990)
  Pallas kernels: 38.4 us -> 37.9 us
    pallas_call x1, Pallas kernels: 38.4 us -> 37.9 us  [on_device(): pl.pallas_call(body, out_shape=jax.ShapeDtypeStruct(head.shape, F32), in_...]
where the time goes in v7:
time: 39.7 us; the launch traced here: 39.6 us
  Pallas kernels  37.9 us (95%)
  local copies, waits for them, and re-layouts  1.67 us (4%)
    pallas_call x1, Pallas kernels, on_device(): pl.pallas_call(body, out_shape=jax.ShapeDtypeStruct(head.shape, F32), in_...  37.9 us
    unnamed x1, local copies, waits for them, and re-layouts  1.67 us

profile of v7, /device:TPU:1, one launch (start us, length us, event | category | flops | bytes accessed | tf_op | source)
XLA Modules:
  0.0 39.6 jit_solution(9390928152116878904)
XLA Ops:
  0.0 37.9 %vcycle.1 = f32[32,16,128]{2,1,0:T(8,128)} custom-call(f32[32,16,128]{2,1,0:T(8,128)} %refs_0_.1, f32[32,16,128]{2,1,0:T(8,128)} %refs_1_.1, f32[32,16,128]{2,1,0:T(8,128)} %refs_2_.1), custom_call_target="tpu_custom_call" | custom-call | tf_op jit(solution)/shard_map/vcycle/pallas_call | solution.py:636
  37.9 1.7 %copy.5 = f32[32,16,128]{2,1,0:T(8,128)} copy(f32[32,16,128]{2,1,0:T(8,128)} %vcycle.1) | data formatting | bytes 524288

commit v8 on v7

--- a/solution.py
+++ b/solution.py
@@ -196,14 +196,14 @@
         wide[:, pl.ds(0, half, stride=2), :] = coarse
         wide[:, pl.ds(1, half, stride=2), :] = coarse
         place = (pl.ds(x0, 2 * count), pl.ds(PAD, rows))
-        copies = jnp.broadcast_to(wide[...][:, None], (count, 2, rows, LANES))
+        copies = jnp.broadcast_to(wide[:, pl.ds(0, rows), :][:, None], (count, 2, rows, LANES))
         v[place] = v[place] + copies.reshape(2 * count, rows, LANES)
 
 
 def restrict(value, half, span, scale):
     x, y, _ = value.shape
     value = value.reshape(x // 2, 2, y, LANES)
-    half[...] = value[:, 0] + value[:, 1]
+    half[:, pl.ds(0, y), :] = value[:, 0] + value[:, 1]
     total = half[:, pl.ds(0, y // 2, stride=2), :] + half[:, pl.ds(1, y // 2, stride=2), :]
     return scale * (total + swap(total, span))
 
@@ -465,7 +465,7 @@
 
     def gather_x(strip, place, stage):
         for k in far_first(gx_size):
-            push(strip, place, stage, k, 0)
+            push(strip.at[pl.ds(0, gy_size), :], place, stage, k, 0)
 
     lv0, lv1, lv2 = SPLIT
     for far in ((True,), (False,)):
@@ -475,7 +475,7 @@
 
     def pack_3(rows):
         lane, row = iota((8, LANES), 1), iota((8, LANES), 0)
-        picked = lane_gather(rows[...], (lane & 15) * 8)
+        picked = lane_gather(rows[pl.ds(0, 8), :], (lane & 15) * 8)
         return jnp.sum(jnp.where((lane >> 4) == row, picked, 0.0), axis=0, keepdims=True)
 
     def to_rows(value, ref):
@@ -491,7 +491,6 @@
     strip_k[pl.ds(gy, 1), :] = pack_3(rows_k)
     exchange(lv1, lv1.hk, 3, one.k, 7, PAD + 8, one.k, 7, PAD + 8)
     exchange(lv2, lv2.hk, 5, two.k, 6, PAD + 6, two.k, 6, PAD + 6)
-
 
     arrived(0, exchange_rows(lv0, lv0.hk))
     zero.faces()
@@ -523,13 +522,13 @@
     gather_y(strip_g, 9)
     arrived(7, gy_size - 1)
     inner = pl.ds(PAD, gy_size)
-    three.k[pl.ds(gx + EDGE, 1), inner, :] = strip_k[...].reshape(1, gy_size, LANES)
+    three.k[pl.ds(gx + EDGE, 1), inner, :] = strip_k[pl.ds(0, gy_size), :].reshape(1, gy_size, LANES)
     gather_x(strip_k, three.k.at[gx + EDGE, inner, :], 8)
     own_g = (pl.ds(5, 8), pl.ds(6, 4))
     wide_g[own_g] = two.g[own_g]
     exchange(lv2, lv2.hg, 6, wide_g, 5, 6, wide_g, 5, 6)
     arrived(9, gy_size - 1)
-    three.g[pl.ds(gx + EDGE, 1)] = strip_g[...].reshape(1, gy_size, LANES)
+    three.g[pl.ds(gx + EDGE, 1)] = strip_g[pl.ds(0, gy_size), :].reshape(1, gy_size, LANES)
     gather_x(strip_g, three.g.at[gx + EDGE], 10)
     arrived(8, (gx_size - 1) * gy_size)
     three.faces()
@@ -613,15 +612,15 @@
     scratch += [
         pltpu.VMEM((16, 16, LANES), F32),
         pltpu.VMEM((12, 16, LANES), F32),
-        pltpu.VMEM((8, 8, LANES), F32),
-        pltpu.VMEM((4, 4, LANES), F32),
+        pltpu.VMEM((8, 16, LANES), F32),
+        pltpu.VMEM((4, 16, LANES), F32),
         pltpu.VMEM((18, 16, LANES), F32),
-        pltpu.VMEM((18, 24, LANES), F32),
-        pltpu.VMEM((12, 24, LANES), F32),
-        pltpu.VMEM((8, LANES), F32),
-        pltpu.VMEM((8, LANES), F32),
-        pltpu.VMEM((gy_size, LANES), F32),
-        pltpu.VMEM((gy_size, LANES), F32),
+        pltpu.VMEM((18, 32, LANES), F32),
+        pltpu.VMEM((12, 32, LANES), F32),
+        pltpu.VMEM((16, LANES), F32),
+        pltpu.VMEM((16, LANES), F32),
+        pltpu.VMEM((gy_size + PAD, LANES), F32),
+        pltpu.VMEM((gy_size + PAD, LANES), F32),
         pltpu.VMEM((gx_size, gy_size, LANES), F32),
         pltpu.VMEM((gy_size, LANES), F32),
         pltpu.VMEM((TALLY_ROWS, LANES), F32),

time: 39.7 us -> 39.7 us (level)
  no operation moved by 1% of the time
where the time goes in v8:
time: 39.7 us; the launch traced here: 39.6 us
  Pallas kernels  37.9 us (95%)
  local copies, waits for them, and re-layouts  1.67 us (4%)
    pallas_call x1, Pallas kernels, on_device(): pl.pallas_call(body, out_shape=jax.ShapeDtypeStruct(head.shape, F32), in_...  37.9 us
    unnamed x1, local copies, waits for them, and re-layouts  1.67 us

profile of v8, /device:TPU:1, one launch (start us, length us, event | category | flops | bytes accessed | tf_op | source)
XLA Modules:
  0.0 39.6 jit_solution(7457380439081115843)
XLA Ops:
  0.0 37.9 %vcycle.1 = f32[32,16,128]{2,1,0:T(8,128)} custom-call(f32[32,16,128]{2,1,0:T(8,128)} %refs_0_.1, f32[32,16,128]{2,1,0:T(8,128)} %refs_1_.1, f32[32,16,128]{2,1,0:T(8,128)} %refs_2_.1), custom_call_target="tpu_custom_call" | custom-call | tf_op jit(solution)/shard_map/vcycle/pallas_call | solution.py:635
  37.9 1.7 %copy.5 = f32[32,16,128]{2,1,0:T(8,128)} copy(f32[32,16,128]{2,1,0:T(8,128)} %vcycle.1) | data formatting | bytes 524288
